TPU v7x, 32 devices: a whole 2x2x4 slice. The times are simulated.
32 devices in a mesh: ep: 8 (over z, y), dp: 4 (over x, core).
Axes of the slice: x: 2, y: 2, z: 4, core: 2. Of those that a mesh axis runs over, the one named last changes fastest.
Arguments:
- tokens: bfloat16 [4, 32, 3584], P(None, ('ep', 'dp')), may hold values from -6 to 6
- route_weight: bfloat16 [4, 32, 2], P(None, ('ep', 'dp')), may hold values from 0.049804688 to 0.5
- expert_ids: int32 [4, 32, 2], P(None, ('ep', 'dp')), may hold values from 0 to 3, all different within a row; in each aligned block of 4 rows (0 to 3, 4 to 7, ..., all dimensions but the last counted through in order) at most 4 rows name the same one
- replica: int32 [4, 32, 2], P(None, ('ep', 'dp')), may hold values from 0 to 1
- placement: int32 [4, 2], replicated, may hold values from 0 to 3, as said below
- w_gate: bfloat16 [8, 3584, 512], P('ep', None, 'dp'), as said below
- w_up: bfloat16 [8, 3584, 512], P('ep', None, 'dp'), as said below
- w_down: bfloat16 [8, 512, 3584], P('ep', 'dp'), as said below
Outputs:
- moe_out: bfloat16 [4, 32, 3584], P(None, ('ep', 'dp'))
- slot_rows: int32 [4, 8], P(None, 'ep')
Inputs may be any that keep to these rules, and one draw needn't show every extreme that they name: `expert_ids`: in each aligned block of 4 rows (the tokens of one ep index at one step), no expert is named by more than 4 tokens; in some blocks one expert is named by exactly 4. `placement`: every slot holds exactly one expert; 0 experts have two different slots, the others have the same slot in both columns. `w_gate`: two slots of one expert hold equal weights. `w_up`: two slots of one expert hold equal weights. `w_down`: two slots of one expert hold equal weights.
All inputs are finite; a program needn't handle non-finite values.
Results may differ from a plain program's by a relative error of at most 0.0059.
Values may be sent and summed in bfloat16 or wider, within the bound.
A program may use at most 128 MiB of HBM per device.

v0:
```python
import jax
import jax.numpy as jnp
from jax import lax
from jax.sharding import PartitionSpec as P


def pick_slots(expert_ids, replica, placement):
    logical = placement.shape[0]
    chosen = jnp.where(replica[..., None] == 0, placement[:, 0], placement[:, 1])
    matches = expert_ids[..., None] == jnp.arange(logical, dtype=jnp.int32)
    return jnp.sum(jnp.where(matches, chosen, 0), axis=-1)


def place_rows(group_slots, slot_count):
    flat_slots = group_slots.reshape(-1)
    matches = (flat_slots[:, None] == jnp.arange(slot_count, dtype=jnp.int32)[None, :]).astype(
        jnp.int32
    )
    earlier = jnp.cumsum(matches, axis=0) - matches
    position = jnp.sum(earlier * matches, axis=1)
    counts = jnp.sum(matches, axis=0)
    return (position.reshape(group_slots.shape), counts)


def pack_rows(rows, slots, slot_count, capacity, top_count):
    position, counts = place_rows(slots, slot_count)
    target = (slots * capacity + position).reshape(-1)
    repeated = jnp.repeat(rows, top_count, axis=0)
    packed = jnp.zeros((slot_count * capacity, rows.shape[1]), rows.dtype).at[target].set(repeated)
    return (packed.reshape(slot_count, capacity, rows.shape[1]), target)


def expert_block(expert_rows, w_gate, w_up, w_down):
    gate_out = jnp.dot(expert_rows, w_gate[0], preferred_element_type=jnp.float32)
    up_out = jnp.dot(expert_rows, w_up[0], preferred_element_type=jnp.float32)
    hidden = (jax.nn.silu(gate_out) * up_out).astype(jnp.bfloat16)
    return jnp.dot(hidden, w_down[0], preferred_element_type=jnp.float32).astype(jnp.bfloat16)


def combine_rows(
    returned, target, weight_rows, row_count, top_count, slot_count, capacity, model_width
):
    paired = returned.reshape(slot_count, 2, capacity, model_width)
    first_half = paired[:, 0].reshape(-1, model_width)[target].astype(jnp.float32)
    second_half = paired[:, 1].reshape(-1, model_width)[target].astype(jnp.float32)
    weighted = (first_half + second_half) * weight_rows.reshape(-1, 1).astype(jnp.float32)
    return jnp.sum(weighted.reshape(row_count, top_count, model_width), axis=1)


def local(tokens, route_weight, expert_ids, replica, placement, w_gate, w_up, w_down):
    steps_total = tokens.shape[0]
    model_width = tokens.shape[2]
    ep_count = lax.axis_size("ep")
    dp_count = lax.axis_size("dp")
    slot_count = ep_count // 2
    logical = placement.shape[0]
    top_count = expert_ids.shape[2]
    own_count = expert_ids.shape[1]
    group_size = own_count * dp_count
    capacity = 2 * ((group_size * top_count + logical) // (2 * logical)) + 2
    own_slots = pick_slots(expert_ids, replica, placement)
    outputs = []
    load_rows = []
    for step_index in range(steps_total):
        group_slots = lax.all_gather(own_slots[step_index], "dp", axis=0, tiled=True)
        group_counts = place_rows(group_slots, slot_count)[1]
        arrived_counts = lax.all_to_all(
            jnp.repeat(group_counts, 2), "ep", split_axis=0, concat_axis=0, tiled=True
        )
        grouped, group_weight = (
            lax.all_gather(tokens[step_index], "dp", axis=0, tiled=True),
            lax.all_gather(route_weight[step_index], "dp", axis=0, tiled=True),
        )
        send_rows, target = pack_rows(grouped, group_slots, slot_count, capacity, top_count)
        arrived = lax.all_to_all(
            jnp.repeat(send_rows, 2, axis=0), "ep", split_axis=0, concat_axis=0, tiled=True
        )
        block_out = expert_block(arrived.reshape(-1, model_width), w_gate, w_up, w_down)
        returned = lax.all_to_all(
            block_out.reshape(ep_count, capacity, model_width),
            "ep",
            split_axis=0,
            concat_axis=0,
            tiled=True,
        )
        partial_tokens = combine_rows(
            returned, target, group_weight, group_size, top_count, slot_count, capacity, model_width
        )
        token_out = lax.psum_scatter(partial_tokens, "dp", scatter_dimension=0, tiled=True)
        outputs.append(token_out.astype(jnp.bfloat16))
        load_rows.append(jnp.sum(arrived_counts).reshape(1))
    return (jnp.stack(outputs), jnp.stack(load_rows))


def solution(mesh):
    return jax.shard_map(
        local,
        mesh=mesh,
        in_specs=(
            P(None, ("ep", "dp"), None),
            P(None, ("ep", "dp"), None),
            P(None, ("ep", "dp"), None),
            P(None, ("ep", "dp"), None),
            P(),
            P("ep", None, "dp"),
            P("ep", None, "dp"),
            P("ep", "dp", None),
        ),
        out_specs=(P(None, ("ep", "dp"), None), P(None, "ep")),
        check_vma=False,
    )
```

profile of v0, /device:TPU:0, one launch (start us, length us, event | category | flops | bytes accessed | tf_op | source)
XLA Modules:
  0.0 239.1 jit_solution(9264039752093960624)
XLA Ops:
  0.7 0.8 slice_bitcast_fusion.13
  2.5 6.0 %all-gather.8 = s32[4,1,2]{2,1,0:T(1,128)S(1)} all-gather(s32[1,1,2]{2,1,0:T(1,128)S(1)} %bitcast.161), channel_id=1, replica_groups=mesh['ep'=8,'dp'=4] {'dp'}, dimensions={0}, use_global_device_ids=true | all-gather | bytes 40 | tf_op jit(solution)/shard_map/all_gather | solution.py:65
  10.8 6.4 %all-to-all-start.8 = ((s32[8,1,1]{2,1,0:T(1,128)}), s32[8,1,1]{2,1,0:T(1,128)S(1)}, u32[]{:S(2)}, u32[]{:S(2)}) async-start(s32[8,1,1]{2,1,0:T(1,128)} %all_to_all.64), calls=%async_computation.8 | async-start | bytes 8192 | tf_op jit(solution)/shard_map/all_to_all | solution.py:67
  17.2 5.0 %all-gather.9 = s32[4,1,2]{2,1,0:T(1,128)S(1)} all-gather(s32[1,1,2]{2,1,0:T(1,128)S(1)} %bitcast.160), channel_id=1, replica_groups=mesh['ep'=8,'dp'=4] {'dp'}, dimensions={0}, use_global_device_ids=true | all-gather | bytes 40 | tf_op jit(solution)/shard_map/all_gather | solution.py:65
  23.1 5.0 %all-gather.10 = s32[4,1,2]{2,1,0:T(1,128)S(1)} all-gather(s32[1,1,2]{2,1,0:T(1,128)S(1)} %bitcast.159), channel_id=1, replica_groups=mesh['ep'=8,'dp'=4] {'dp'}, dimensions={0}, use_global_device_ids=true | all-gather | bytes 40 | tf_op jit(solution)/shard_map/all_gather | solution.py:65
  28.9 5.0 %all-gather.11 = s32[4,1,2]{2,1,0:T(1,128)S(1)} all-gather(s32[1,1,2]{2,1,0:T(1,128)S(1)} %bitcast.158), channel_id=1, replica_groups=mesh['ep'=8,'dp'=4] {'dp'}, dimensions={0}, use_global_device_ids=true | all-gather | bytes 40 | tf_op jit(solution)/shard_map/all_gather | solution.py:65
  35.5 5.3 %all-gather.2 = bf16[4,1,3584]{2,1,0:T(2,128)(2,1)S(1)} all-gather(bf16[1,1,3584]{2,1,0:T(2,128)(2,1)S(1)} %get-tuple-element.28), channel_id=4, replica_groups=mesh['ep'=8,'dp'=4] {'dp'}, dimensions={0}, use_global_device_ids=true | all-gather | bytes 35840 | tf_op jit(solution)/shard_map/all_gather | solution.py:71
  42.4 5.0 %all-gather.3 = bf16[4,1,2]{2,1,0:T(2,128)(2,1)S(1)} all-gather(bf16[1,1,2]{2,1,0:T(2,128)(2,1)S(1)} %copy.284), channel_id=5, replica_groups=mesh['ep'=8,'dp'=4] {'dp'}, dimensions={0}, use_global_device_ids=true | all-gather | bytes 20 | tf_op jit(solution)/shard_map/all_gather | solution.py:72
  48.6 5.2 %all-gather = bf16[4,1,3584]{2,1,0:T(2,128)(2,1)S(1)} all-gather(bf16[1,1,3584]{2,1,0:T(2,128)(2,1)S(1)} %get-tuple-element.26), channel_id=2, replica_groups=mesh['ep'=8,'dp'=4] {'dp'}, dimensions={0}, use_global_device_ids=true | all-gather | bytes 35840 | tf_op jit(solution)/shard_map/all_gather | solution.py:71
  54.8 5.0 %all-gather.1 = bf16[4,1,2]{2,1,0:T(2,128)(2,1)S(1)} all-gather(bf16[1,1,2]{2,1,0:T(2,128)(2,1)S(1)} %copy.280), channel_id=3, replica_groups=mesh['ep'=8,'dp'=4] {'dp'}, dimensions={0}, use_global_device_ids=true | all-gather | bytes 20 | tf_op jit(solution)/shard_map/all_gather | solution.py:72
  61.4 5.2 %all-gather.4 = bf16[4,1,3584]{2,1,0:T(2,128)(2,1)S(1)} all-gather(bf16[1,1,3584]{2,1,0:T(2,128)(2,1)S(1)} %get-tuple-element.27), channel_id=6, replica_groups=mesh['ep'=8,'dp'=4] {'dp'}, dimensions={0}, use_global_device_ids=true | all-gather | bytes 35840 | tf_op jit(solution)/shard_map/all_gather | solution.py:71
  67.6 5.0 %all-gather.5 = bf16[4,1,2]{2,1,0:T(2,128)(2,1)S(1)} all-gather(bf16[1,1,2]{2,1,0:T(2,128)(2,1)S(1)} %copy.288), channel_id=7, replica_groups=mesh['ep'=8,'dp'=4] {'dp'}, dimensions={0}, use_global_device_ids=true | all-gather | bytes 20 | tf_op jit(solution)/shard_map/all_gather | solution.py:72
  74.2 5.2 %all-gather.6 = bf16[4,1,3584]{2,1,0:T(2,128)(2,1)S(1)} all-gather(bf16[1,1,3584]{2,1,0:T(2,128)(2,1)S(1)} %get-tuple-element.29), channel_id=8, replica_groups=mesh['ep'=8,'dp'=4] {'dp'}, dimensions={0}, use_global_device_ids=true | all-gather | bytes 35840 | tf_op jit(solution)/shard_map/all_gather | solution.py:71
  81.0 5.0 %all-gather.7 = bf16[4,1,2]{2,1,0:T(2,128)(2,1)S(1)} all-gather(bf16[1,1,2]{2,1,0:T(2,128)(2,1)S(1)} %copy.292), channel_id=9, replica_groups=mesh['ep'=8,'dp'=4] {'dp'}, dimensions={0}, use_global_device_ids=true | all-gather | bytes 20 | tf_op jit(solution)/shard_map/all_gather | solution.py:72
  89.0 6.0 %all-to-all-start.9 = ((s32[8,1,1]{2,1,0:T(1,128)}), s32[8,1,1]{2,1,0:T(1,128)S(1)}, u32[]{:S(2)}, u32[]{:S(2)}) async-start(s32[8,1,1]{2,1,0:T(1,128)} %all_to_all.65), calls=%async_computation.9 | async-start | bytes 8192 | tf_op jit(solution)/shard_map/all_to_all | solution.py:67
  95.0 6.5 %all-to-all-done.9 = s32[8,1,1]{2,1,0:T(1,128)S(1)} async-done(((s32[8,1,1]{2,1,0:T(1,128)}), s32[8,1,1]{2,1,0:T(1,128)S(1)}, u32[]{:S(2)}, u32[]{:S(2)}) %all-to-all-start.9) | async-done | bytes 64 | tf_op jit(solution)/shard_map/all_to_all | solution.py:67
  101.5 3.3 %all-to-all-start.10 = ((s32[8,1,1]{2,1,0:T(1,128)}), s32[8,1,1]{2,1,0:T(1,128)S(1)}, u32[]{:S(2)}, u32[]{:S(2)}) async-start(s32[8,1,1]{2,1,0:T(1,128)} %all_to_all.66), calls=%async_computation.10 | async-start | bytes 8192 | tf_op jit(solution)/shard_map/all_to_all | solution.py:67
  104.8 6.4 %all-to-all-done.10 = s32[8,1,1]{2,1,0:T(1,128)S(1)} async-done(((s32[8,1,1]{2,1,0:T(1,128)}), s32[8,1,1]{2,1,0:T(1,128)S(1)}, u32[]{:S(2)}, u32[]{:S(2)}) %all-to-all-start.10) | async-done | bytes 64 | tf_op jit(solution)/shard_map/all_to_all | solution.py:67
  111.2 3.3 %all-to-all-start.11 = ((s32[8,1,1]{2,1,0:T(1,128)}), s32[8,1,1]{2,1,0:T(1,128)S(1)}, u32[]{:S(2)}, u32[]{:S(2)}) async-start(s32[8,1,1]{2,1,0:T(1,128)} %all_to_all.67), calls=%async_computation.11 | async-start | bytes 8192 | tf_op jit(solution)/shard_map/all_to_all | solution.py:67
  115.1 5.7 %all-to-all-done.11 = s32[8,1,1]{2,1,0:T(1,128)S(1)} async-done(((s32[8,1,1]{2,1,0:T(1,128)}), s32[8,1,1]{2,1,0:T(1,128)S(1)}, u32[]{:S(2)}, u32[]{:S(2)}) %all-to-all-start.11) | async-done | bytes 64 | tf_op jit(solution)/shard_map/all_to_all | solution.py:67
  121.5 3.5 %all-to-all-start.2 = ((bf16[8,4,3584]{2,1,0:T(4,128)(2,1)}), bf16[8,4,3584]{2,1,0:T(4,128)(2,1)S(1)}, u32[]{:S(2)}, u32[]{:S(2)}) async-start(bf16[8,4,3584]{2,1,0:T(4,128)(2,1)} %bitcast.15), calls=%async_computation.2 | async-start | bytes 458752 | tf_op jit(solution)/shard_map/all_to_all | solution.py:75
  129.5 3.0 %pad_add_fusion = s32[4,1]{0,1:T(1,128)} fusion(s32[1,1]{0,1:T(1,128)} %bitcast.34, s32[1,1]{0,1:T(1,128)} %bitcast.33, s32[1,1]{0,1:T(1,128)} %bitcast.32, s32[1,1]{0,1:T(1,128)} %bitcast.31), kind=kLoop, calls=%fused_computation.144 | loop fusion | flops 12 | bytes 32 | tf_op jit(solution)/shard_map/stack | solution.py:92
  133.8 5.4 %all-to-all-start = ((bf16[8,4,3584]{2,1,0:T(4,128)(2,1)}), bf16[8,4,3584]{2,1,0:T(4,128)(2,1)S(1)}, u32[]{:S(2)}, u32[]{:S(2)}) async-start(bf16[8,4,3584]{2,1,0:T(4,128)(2,1)} %bitcast.6), calls=%async_computation | async-start | bytes 458752 | tf_op jit(solution)/shard_map/all_to_all | solution.py:75
  139.3 0.9 fusion.20
  140.4 1.2 convolution_convert_fusion.2
  141.6 5.6 %all-to-all-done = bf16[8,4,3584]{2,1,0:T(4,128)(2,1)S(1)} async-done(((bf16[8,4,3584]{2,1,0:T(4,128)(2,1)}), bf16[8,4,3584]{2,1,0:T(4,128)(2,1)S(1)}, u32[]{:S(2)}, u32[]{:S(2)}) %all-to-all-start) | async-done | bytes 229408 | tf_op jit(solution)/shard_map/all_to_all | solution.py:75
  147.2 0.8 broadcast_in_dim.88
  148.0 4.0 %all-to-all-start.4 = ((bf16[8,4,3584]{2,1,0:T(4,128)(2,1)}), bf16[8,4,3584]{2,1,0:T(4,128)(2,1)}, u32[]{:S(2)}, u32[]{:S(2)}) async-start(bf16[8,4,3584]{2,1,0:T(4,128)(2,1)} %bitcast.21), calls=%async_computation.4 | async-start | bytes 458752 | tf_op jit(solution)/shard_map/all_to_all | solution.py:75
  152.0 1.0 reshape.348
  153.0 0.9 fusion.22
  153.9 1.2 convolution_convert_fusion.3
  155.1 4.9 %all-to-all-done.4 = bf16[8,4,3584]{2,1,0:T(4,128)(2,1)} async-done(((bf16[8,4,3584]{2,1,0:T(4,128)(2,1)}), bf16[8,4,3584]{2,1,0:T(4,128)(2,1)}, u32[]{:S(2)}, u32[]{:S(2)}) %all-to-all-start.4) | async-done | bytes 229408 | tf_op jit(solution)/shard_map/all_to_all | solution.py:75
  160.8 4.0 %all-to-all-start.6 = ((bf16[8,4,3584]{2,1,0:T(4,128)(2,1)}), bf16[8,4,3584]{2,1,0:T(4,128)(2,1)}, u32[]{:S(2)}, u32[]{:S(2)}) async-start(bf16[8,4,3584]{2,1,0:T(4,128)(2,1)} %bitcast.27), calls=%async_computation.6 | async-start | bytes 458752 | tf_op jit(solution)/shard_map/all_to_all | solution.py:75
  164.8 1.0 reshape.364
  166.1 0.8 reshape.357
  167.3 5.5 %all-to-all-done.6 = bf16[8,4,3584]{2,1,0:T(4,128)(2,1)} async-done(((bf16[8,4,3584]{2,1,0:T(4,128)(2,1)}), bf16[8,4,3584]{2,1,0:T(4,128)(2,1)}, u32[]{:S(2)}, u32[]{:S(2)}) %all-to-all-start.6) | async-done | bytes 229408 | tf_op jit(solution)/shard_map/all_to_all | solution.py:75
  172.9 4.0 %all-to-all-start.3 = ((bf16[8,4,3584]{2,1,0:T(4,128)(2,1)}), bf16[8,4,3584]{2,1,0:T(4,128)(2,1)}, u32[]{:S(2)}, u32[]{:S(2)}) async-start(bf16[8,4,3584]{2,1,0:T(4,128)(2,1)} %reshape.357), calls=%async_computation.3 | async-start | bytes 458752 | tf_op jit(solution)/shard_map/all_to_all | solution.py:79
  176.9 1.0 reshape.372
  178.2 0.8 reshape.349
  180.9 4.0 %all-to-all-done.3 = bf16[8,4,3584]{2,1,0:T(4,128)(2,1)} async-done(((bf16[8,4,3584]{2,1,0:T(4,128)(2,1)}), bf16[8,4,3584]{2,1,0:T(4,128)(2,1)}, u32[]{:S(2)}, u32[]{:S(2)}) %all-to-all-start.3) | async-done | bytes 229408 | tf_op jit(solution)/shard_map/all_to_all | solution.py:79
  184.9 4.4 %all-to-all-start.1 = ((bf16[8,4,3584]{2,1,0:T(4,128)(2,1)}), bf16[8,4,3584]{2,1,0:T(4,128)(2,1)S(1)}, u32[]{:S(2)}, u32[]{:S(2)}) async-start(bf16[8,4,3584]{2,1,0:T(4,128)(2,1)} %reshape.349), calls=%async_computation.1 | async-start | bytes 458752 | tf_op jit(solution)/shard_map/all_to_all | solution.py:79
  189.4 1.0 slice_bitcast_fusion.5
  190.4 8.4 %all-to-all-done.1 = bf16[8,4,3584]{2,1,0:T(4,128)(2,1)S(1)} async-done(((bf16[8,4,3584]{2,1,0:T(4,128)(2,1)}), bf16[8,4,3584]{2,1,0:T(4,128)(2,1)S(1)}, u32[]{:S(2)}, u32[]{:S(2)}) %all-to-all-start.1) | async-done | bytes 229408 | tf_op jit(solution)/shard_map/all_to_all | solution.py:79
  198.8 3.4 %all-to-all-start.5 = ((bf16[8,4,3584]{2,1,0:T(4,128)(2,1)}), bf16[8,4,3584]{2,1,0:T(4,128)(2,1)S(1)}, u32[]{:S(2)}, u32[]{:S(2)}) async-start(bf16[8,4,3584]{2,1,0:T(4,128)(2,1)} %reshape.365), calls=%async_computation.5 | async-start | bytes 458752 | tf_op jit(solution)/shard_map/all_to_all | solution.py:79
  205.3 5.5 %all-to-all-done.5 = bf16[8,4,3584]{2,1,0:T(4,128)(2,1)S(1)} async-done(((bf16[8,4,3584]{2,1,0:T(4,128)(2,1)}), bf16[8,4,3584]{2,1,0:T(4,128)(2,1)S(1)}, u32[]{:S(2)}, u32[]{:S(2)}) %all-to-all-start.5) | async-done | bytes 229408 | tf_op jit(solution)/shard_map/all_to_all | solution.py:79
  210.8 3.4 %all-to-all-start.7 = ((bf16[8,4,3584]{2,1,0:T(4,128)(2,1)}), bf16[8,4,3584]{2,1,0:T(4,128)(2,1)S(1)}, u32[]{:S(2)}, u32[]{:S(2)}) async-start(bf16[8,4,3584]{2,1,0:T(4,128)(2,1)} %reshape.373), calls=%async_computation.7 | async-start | bytes 458752 | tf_op jit(solution)/shard_map/all_to_all | solution.py:79
  218.5 3.6 %all-to-all-done.7 = bf16[8,4,3584]{2,1,0:T(4,128)(2,1)S(1)} async-done(((bf16[8,4,3584]{2,1,0:T(4,128)(2,1)}), bf16[8,4,3584]{2,1,0:T(4,128)(2,1)S(1)}, u32[]{:S(2)}, u32[]{:S(2)}) %all-to-all-start.7) | async-done | bytes 229408 | tf_op jit(solution)/shard_map/all_to_all | solution.py:79
  224.6 12.6 %all-reduce.6 = (bf16[4,3584]{1,0:T(4,128)(2,1)S(1)}, bf16[4,3584]{1,0:T(4,128)(2,1)S(1)}, bf16[4,3584]{1,0:T(4,128)(2,1)S(1)}, bf16[4,3584]{1,0:T(4,128)(2,1)S(1)}) all-reduce(f32[4,3584]{1,0:T(4,128)S(1)} %multiply_reduce_fusion, f32[4,3584]{1,0:T(4,128)S(1)} %multiply_reduce_fusion.1, ...), channel_id=13, replica_groups=mesh['ep'=8,'dp'=4] {'dp'}, use_global_device_ids=true, to_apply=%region_20.21.clone | all-reduce | flops 57344 | bytes 344064
  (181 shorter events, 41.5 us)
Async XLA Ops:
  0.6 139.5 %copy-start = (bf16[1,128,3584]{2,1,0:T(8,128)(2,1)S(1)}, bf16[1,128,3584]{2,1,0:T(8,128)(2,1)}, u32[]{:S(2)}) copy-start(bf16[1,128,3584]{2,1,0:T(8,128)(2,1)} %param.15) | copy-start | bytes 2752516
  0.6 0.8 copy-start.12
  1.4 0.7 copy-start.11
  10.8 78.2 %all-to-all-start.8 = ((s32[8,1,1]{2,1,0:T(1,128)}), s32[8,1,1]{2,1,0:T(1,128)S(1)}, u32[]{:S(2)}, u32[]{:S(2)}) async-start(s32[8,1,1]{2,1,0:T(1,128)} %all_to_all.64), calls=%async_computation.8 | async-start | bytes 8192 | tf_op jit(solution)/shard_map/all_to_all | solution.py:67
  28.8 6.7 %copy-start.5 = (bf16[4,1,3584]{2,0,1:T(4,128)(2,1)S(1)}, bf16[4,1,3584]{2,0,1:T(4,128)(2,1)}, u32[]{:S(2)}) copy-start(bf16[4,1,3584]{2,0,1:T(4,128)(2,1)} %param.8) | copy-start | bytes 86020
  40.8 0.7 copy-start.10
  89.0 12.5 %all-to-all-start.9 = ((s32[8,1,1]{2,1,0:T(1,128)}), s32[8,1,1]{2,1,0:T(1,128)S(1)}, u32[]{:S(2)}, u32[]{:S(2)}) async-start(s32[8,1,1]{2,1,0:T(1,128)} %all_to_all.65), calls=%async_computation.9 | async-start | bytes 8192 | tf_op jit(solution)/shard_map/all_to_all | solution.py:67
  101.5 9.7 %all-to-all-start.10 = ((s32[8,1,1]{2,1,0:T(1,128)}), s32[8,1,1]{2,1,0:T(1,128)S(1)}, u32[]{:S(2)}, u32[]{:S(2)}) async-start(s32[8,1,1]{2,1,0:T(1,128)} %all_to_all.66), calls=%async_computation.10 | async-start | bytes 8192 | tf_op jit(solution)/shard_map/all_to_all | solution.py:67
  104.8 9.7 %copy-start.13 = (u32[32]{0:T(128)S(1)}, u32[32]{0:T(128)}, u32[]{:S(2)}) copy-start(u32[32]{0:T(128)} %constant.37) | copy-start | bytes 388
  111.2 9.6 %all-to-all-start.11 = ((s32[8,1,1]{2,1,0:T(1,128)}), s32[8,1,1]{2,1,0:T(1,128)S(1)}, u32[]{:S(2)}, u32[]{:S(2)}) async-start(s32[8,1,1]{2,1,0:T(1,128)} %all_to_all.67), calls=%async_computation.11 | async-start | bytes 8192 | tf_op jit(solution)/shard_map/all_to_all | solution.py:67
  121.5 17.7 %copy-start.2 = (bf16[1,3584,128]{2,1,0:T(8,128)(2,1)S(1)}, bf16[1,3584,128]{2,1,0:T(8,128)(2,1)}, u32[]{:S(2)}) copy-start(bf16[1,3584,128]{2,1,0:T(8,128)(2,1)} %param.13) | copy-start | bytes 2752516
  121.5 11.5 %all-to-all-start.2 = ((bf16[8,4,3584]{2,1,0:T(4,128)(2,1)}), bf16[8,4,3584]{2,1,0:T(4,128)(2,1)S(1)}, u32[]{:S(2)}, u32[]{:S(2)}) async-start(bf16[8,4,3584]{2,1,0:T(4,128)(2,1)} %bitcast.15), calls=%async_computation.2 | async-start | bytes 458752 | tf_op jit(solution)/shard_map/all_to_all | solution.py:75
  133.8 13.4 %all-to-all-start = ((bf16[8,4,3584]{2,1,0:T(4,128)(2,1)}), bf16[8,4,3584]{2,1,0:T(4,128)(2,1)S(1)}, u32[]{:S(2)}, u32[]{:S(2)}) async-start(bf16[8,4,3584]{2,1,0:T(4,128)(2,1)} %bitcast.6), calls=%async_computation | async-start | bytes 458752 | tf_op jit(solution)/shard_map/all_to_all | solution.py:75
  139.2 1.2 copy-start.1
  147.2 0.8 copy-start.3
  148.0 12.1 %all-to-all-start.4 = ((bf16[8,4,3584]{2,1,0:T(4,128)(2,1)}), bf16[8,4,3584]{2,1,0:T(4,128)(2,1)}, u32[]{:S(2)}, u32[]{:S(2)}) async-start(bf16[8,4,3584]{2,1,0:T(4,128)(2,1)} %bitcast.21), calls=%async_computation.4 | async-start | bytes 458752 | tf_op jit(solution)/shard_map/all_to_all | solution.py:75
  153.9 6.2 %copy-start.4 = (bf16[4,4,3584]{2,1,0:T(4,128)(2,1)S(1)}, bf16[4,4,3584]{2,1,0:T(4,128)(2,1)}, u32[]{:S(2)}) copy-start(bf16[4,4,3584]{2,1,0:T(4,128)(2,1)} %reshape.370) | copy-start | bytes 344068
  160.8 12.1 %all-to-all-start.6 = ((bf16[8,4,3584]{2,1,0:T(4,128)(2,1)}), bf16[8,4,3584]{2,1,0:T(4,128)(2,1)}, u32[]{:S(2)}, u32[]{:S(2)}) async-start(bf16[8,4,3584]{2,1,0:T(4,128)(2,1)} %bitcast.27), calls=%async_computation.6 | async-start | bytes 458752 | tf_op jit(solution)/shard_map/all_to_all | solution.py:75
  172.9 12.1 %all-to-all-start.3 = ((bf16[8,4,3584]{2,1,0:T(4,128)(2,1)}), bf16[8,4,3584]{2,1,0:T(4,128)(2,1)}, u32[]{:S(2)}, u32[]{:S(2)}) async-start(bf16[8,4,3584]{2,1,0:T(4,128)(2,1)} %reshape.357), calls=%async_computation.3 | async-start | bytes 458752 | tf_op jit(solution)/shard_map/all_to_all | solution.py:79
  184.9 13.8 %all-to-all-start.1 = ((bf16[8,4,3584]{2,1,0:T(4,128)(2,1)}), bf16[8,4,3584]{2,1,0:T(4,128)(2,1)S(1)}, u32[]{:S(2)}, u32[]{:S(2)}) async-start(bf16[8,4,3584]{2,1,0:T(4,128)(2,1)} %reshape.349), calls=%async_computation.1 | async-start | bytes 458752 | tf_op jit(solution)/shard_map/all_to_all | solution.py:79
  198.8 12.0 %all-to-all-start.5 = ((bf16[8,4,3584]{2,1,0:T(4,128)(2,1)}), bf16[8,4,3584]{2,1,0:T(4,128)(2,1)S(1)}, u32[]{:S(2)}, u32[]{:S(2)}) async-start(bf16[8,4,3584]{2,1,0:T(4,128)(2,1)} %reshape.365), calls=%async_computation.5 | async-start | bytes 458752 | tf_op jit(solution)/shard_map/all_to_all | solution.py:79
  210.8 11.4 %all-to-all-start.7 = ((bf16[8,4,3584]{2,1,0:T(4,128)(2,1)}), bf16[8,4,3584]{2,1,0:T(4,128)(2,1)S(1)}, u32[]{:S(2)}, u32[]{:S(2)}) async-start(bf16[8,4,3584]{2,1,0:T(4,128)(2,1)} %reshape.373), calls=%async_computation.7 | async-start | bytes 458752 | tf_op jit(solution)/shard_map/all_to_all | solution.py:79
  215.8 0.7 copy-start.6
  216.7 0.7 copy-start.7
  217.6 0.7 copy-start.8
  223.8 0.7 copy-start.9
where the time goes:
time: 241 us; the launch traced here: 239 us
  blocking collectives  74.7 us (31%)
  waiting for transfers between devices  56.6 us (23%)
  starting transfers between devices  51.3 us (21%)
  local copies, waits for them, and re-layouts  35.8 us (15%)
  other arithmetic  13.8 us (6%)
  matrix products  5.62 us (2%)
    all_to_all x4, waiting for transfers between devices, local(): lax.all_to_all(block_out.reshape(ep_count, capacity, model_width), 'ep',...  21.5 us
    all_gather x4, blocking collectives, local(): lax.all_gather(own_slots[step_index], 'dp', axis=0, tiled=True)  21 us
    all_gather x4, blocking collectives, local(): lax.all_gather(tokens[step_index], 'dp', axis=0, tiled=True)  21 us
    all_gather x4, blocking collectives, local(): lax.all_gather(route_weight[step_index], 'dp', axis=0, tiled=True)  20.2 us
    all_to_all x4, starting transfers between devices, local(): lax.all_to_all(jnp.repeat(group_counts, 2), 'ep', split_axis=0, concat_ax...  19 us
    all_to_all x4, waiting for transfers between devices, local(): lax.all_to_all(jnp.repeat(group_counts, 2), 'ep', split_axis=0, concat_ax...  18.6 us
    all_to_all x4, starting transfers between devices, local(): lax.all_to_all(jnp.repeat(send_rows, 2, axis=0), 'ep', split_axis=0, conc...  17 us
    all_to_all x4, waiting for transfers between devices, local(): lax.all_to_all(jnp.repeat(send_rows, 2, axis=0), 'ep', split_axis=0, conc...  16.5 us
  transfers between devices with their start and end apart: 12, of which 11 were waited for; matrix products, arithmetic and copies ran while one was open for 17% of the time, Pallas kernels for 0%

commit v1 on v0

--- a/solution.py
+++ b/solution.py
@@ -1,7 +1,14 @@
+import functools
+
 import jax
 import jax.numpy as jnp
 from jax import lax
+from jax.experimental import pallas as pl
+from jax.experimental.pallas import tpu as pltpu
 from jax.sharding import PartitionSpec as P
+
+MESH = pl.DeviceIdType.MESH
+LANES = 128
 
 
 def pick_slots(expert_ids, replica, placement):
@@ -47,7 +54,7 @@
     return jnp.sum(weighted.reshape(row_count, top_count, model_width), axis=1)
 
 
-def local(tokens, route_weight, expert_ids, replica, placement, w_gate, w_up, w_down):
+def local_packed(tokens, route_weight, expert_ids, replica, placement, w_gate, w_up, w_down):
     steps_total = tokens.shape[0]
     model_width = tokens.shape[2]
     ep_count = lax.axis_size("ep")
@@ -92,9 +99,219 @@
     return (jnp.stack(outputs), jnp.stack(load_rows))
 
 
+def moe_kernel(
+    steps,
+    msg_ref,
+    w_gate_ref,
+    w_up_ref,
+    w_down_ref,
+    out_ref,
+    count_ref,
+    wgu,
+    wd,
+    zbuf,
+    gx,
+    ps,
+    cs,
+    cr,
+    first_s,
+    second_s,
+    first_r,
+    second_r,
+    tbuf,
+    zr,
+    wsem,
+    ssem,
+    rsem,
+):
+    ep, dp = lax.axis_index("ep"), lax.axis_index("dp")
+    z, y = ep // 2, ep % 2
+    x, c = dp // 2, dp % 2
+    width = wgu.shape[0]
+    cols = width // LANES
+    rows_own = cols * steps
+    hid = w_gate_ref.shape[2]
+    f32, bf16 = jnp.float32, jnp.bfloat16
+
+    loads = [
+        pltpu.make_async_copy(w_gate_ref.at[0], wgu.at[:, pl.ds(0, hid)], wsem.at[0]),
+        pltpu.make_async_copy(w_up_ref.at[0], wgu.at[:, pl.ds(hid, hid)], wsem.at[1]),
+        pltpu.make_async_copy(w_down_ref.at[0], wd, wsem.at[2]),
+    ]
+    for load in loads:
+        load.start()
+
+    def device(zz, yy, xx, cc):
+        return (zz * 2 + yy, xx * 2 + cc)
+
+    z_others = [z + 1 - 2 * (z % 2), (z + 2) % 4, 3 - z]
+    z_dev = [device(zz, y, x, c) for zz in z_others]
+    core_dev = device(z, y, x, 1 - c)
+    first_dev = device(z, y + c * (1 - 2 * y), x + (1 - c) * (1 - 2 * x), c)
+    second_dev = device(z, y + (1 - c) * (1 - 2 * y), x + c * (1 - 2 * x), c)
+    slot_a, slot_b = 2 - c, 1 + c
+
+    barrier = pltpu.get_barrier_semaphore()
+    partners = z_dev + [core_dev, first_dev, second_dev]
+    for partner in partners:
+        pl.semaphore_signal(barrier, inc=1, device_id=partner, device_id_type=MESH)
+    pl.semaphore_wait(barrier, len(partners))
+
+    started = []
+
+    def send(src, dst, to):
+        n = len(started)
+        copy = pltpu.make_async_remote_copy(
+            src_ref=src,
+            dst_ref=dst,
+            send_sem=ssem.at[n],
+            recv_sem=rsem.at[n],
+            device_id=to,
+            device_id_type=MESH,
+        )
+        copy.start()
+        started.append(copy)
+        return copy
+
+    z_in = [send(msg_ref, zbuf.at[k + 1], z_dev[k]) for k in (2, 1, 0)]
+    zbuf[0] = msg_ref[...]
+    per = zbuf.shape[1]
+    block = 4 * steps
+    r = lax.broadcasted_iota(jnp.int32, ((cols + 1) * block, 4 * per), 0)
+    q = lax.broadcasted_iota(jnp.int32, ((cols + 1) * block, 4 * per), 1)
+    source = (r % block) // steps * per + r // block * steps + r % steps
+    spread = jnp.where(source == q, 1.0, 0.0).astype(bf16)
+    for copy in z_in:
+        copy.wait_recv()
+    mixed = jnp.dot(spread, zbuf[...].reshape(4 * per, LANES), preferred_element_type=f32)
+    mixed = mixed.astype(bf16)
+    for j in range(cols + 1):
+        gx[0, :, j * LANES : (j + 1) * LANES] = mixed[j * block : (j + 1) * block]
+
+    own_a = send(gx.at[0], gx.at[slot_a], first_dev)
+    own_b = send(gx.at[0], gx.at[slot_b], second_dev)
+    from_core = [send(gx.at[0], gx.at[4], core_dev)]
+    own_a.wait_recv()
+    diag = send(gx.at[slot_a], gx.at[3], second_dev)
+    from_core.append(send(gx.at[slot_a], gx.at[4 + slot_a], core_dev))
+    own_b.wait_recv()
+    from_core.append(send(gx.at[slot_b], gx.at[4 + slot_b], core_dev))
+    diag.wait_recv()
+    from_core.append(send(gx.at[3], gx.at[7], core_dev))
+    for load in loads:
+        load.wait()
+    for copy in from_core:
+        copy.wait_recv()
+
+    total = 8 * block
+    tokens = gx[:, :, 0:width].reshape(total, width)
+    both = jnp.dot(tokens, wgu[...], preferred_element_type=f32)
+    gate, up = both[:, :hid], both[:, hid:]
+    hidden = (gate / (1.0 + jnp.exp(-gate)) * up).astype(bf16)
+    route = gx[:, :, width : width + LANES].reshape(total, LANES).astype(f32)
+    lane = lax.broadcasted_iota(jnp.int32, (total, LANES), 1)
+    weight = jnp.sum(jnp.where(lane == z, route, 0.0), axis=1, keepdims=True)
+    counted = jnp.sum(jnp.where(lane == z + 4, route, 0.0), axis=1, keepdims=True)
+    row = lax.broadcasted_iota(jnp.int32, (total, LANES), 0)
+    per_step = jnp.where(lane == row % steps, counted, 0.0)
+    count_ref[...] = jnp.sum(per_step, axis=0, keepdims=True).astype(jnp.int32)
+
+    half = total // 2
+    theirs = jnp.dot(hidden[half:], wd[...], preferred_element_type=f32) * weight[half:]
+    cs[...] = theirs.astype(bf16).reshape(4, block, width)
+    to_core = send(cs, cr, core_dev)
+    mine = jnp.dot(hidden[:half], wd[...], preferred_element_type=f32) * weight[:half]
+    ps[...] = mine.reshape(4, block, width)
+    to_core.wait_recv()
+
+    first_s[0] = (ps[3] + cr[3].astype(f32)).astype(bf16)
+    diag_out = send(first_s.at[0], first_r.at[0], first_dev)
+    first_s[1] = (ps[slot_a] + cr[slot_a].astype(f32)).astype(bf16)
+    first_out = send(first_s.at[1], first_r.at[1], first_dev)
+    held = ps[slot_b] + cr[slot_b].astype(f32)
+    diag_out.wait_recv()
+    second_s[...] = (held + first_r[0].astype(f32)).astype(bf16)
+    second_out = send(second_s, second_r, second_dev)
+    held = ps[0] + cr[0].astype(f32)
+    first_out.wait_recv()
+    held = held + first_r[1].astype(f32)
+    r = lax.broadcasted_iota(jnp.int32, (4 * rows_own, cols * block), 0)
+    q = lax.broadcasted_iota(jnp.int32, (4 * rows_own, cols * block), 1)
+    source = (r % rows_own) // steps * block + r // rows_own * steps + r % steps
+    gather = jnp.where(source == q, 1.0, 0.0).astype(bf16)
+    second_out.wait_recv()
+    summed = (held + second_r[...].astype(f32)).astype(bf16)
+    stacked = jnp.concatenate(
+        [summed[:, j * LANES : (j + 1) * LANES] for j in range(cols)], axis=0
+    )
+    split = jnp.dot(gather, stacked, preferred_element_type=f32)
+    tbuf[...] = split.astype(bf16).reshape(4, rows_own, LANES)
+    z_out = [send(tbuf.at[k + 1], zr.at[k], z_dev[k]) for k in (2, 1, 0)]
+    final = tbuf[0].astype(f32)
+    for copy in z_out:
+        copy.wait_recv()
+    for k in range(3):
+        final = final + zr[k].astype(f32)
+    out_ref[...] = final
+    for copy in started:
+        copy.wait_send()
+
+
+def local_gathered(tokens, route_weight, expert_ids, replica, placement, w_gate, w_up, w_down):
+    steps, own, width = tokens.shape
+    hid = w_gate.shape[2]
+    cols = width // LANES
+    slots = pick_slots(expert_ids, replica, placement)[:, 0, :]
+    hits = slots[:, :, None] == jnp.arange(4, dtype=jnp.int32)
+    weights = jnp.sum(jnp.where(hits, route_weight[:, 0, :, None].astype(jnp.float32), 0.0), axis=1)
+    counts = jnp.sum(hits.astype(jnp.float32), axis=1)
+    extra = jnp.concatenate([weights, counts], axis=1).astype(jnp.bfloat16)
+    extra = jnp.pad(extra, ((0, 16 - steps), (0, LANES - 8)))
+    rows = tokens.reshape(steps, cols, LANES).transpose(1, 0, 2).reshape(cols * steps, LANES)
+    message = jnp.concatenate([rows, extra], axis=0)
+    per = message.shape[0]
+    block = 4 * steps
+    bf16 = jnp.bfloat16
+    vmem = pl.BlockSpec(memory_space=pltpu.VMEM)
+    anywhere = pl.BlockSpec(memory_space=pl.ANY)
+    out, count = pl.pallas_call(
+        functools.partial(moe_kernel, steps),
+        out_shape=(
+            jax.ShapeDtypeStruct((cols * steps, LANES), jnp.float32),
+            jax.ShapeDtypeStruct((1, LANES), jnp.int32),
+        ),
+        in_specs=[vmem, anywhere, anywhere, anywhere],
+        out_specs=(vmem, vmem),
+        scratch_shapes=[
+            pltpu.VMEM((width, 2 * hid), bf16),
+            pltpu.VMEM((hid, width), bf16),
+            pltpu.VMEM((4, per, LANES), bf16),
+            pltpu.VMEM((8, block, width + LANES), bf16),
+            pltpu.VMEM((4, block, width), jnp.float32),
+            pltpu.VMEM((4, block, width), bf16),
+            pltpu.VMEM((4, block, width), bf16),
+            pltpu.VMEM((2, block, width), bf16),
+            pltpu.VMEM((block, width), bf16),
+            pltpu.VMEM((2, block, width), bf16),
+            pltpu.VMEM((block, width), bf16),
+            pltpu.VMEM((4, cols * steps, LANES), bf16),
+            pltpu.VMEM((3, cols * steps, LANES), bf16),
+            pltpu.SemaphoreType.DMA((3,)),
+            pltpu.SemaphoreType.DMA((18,)),
+            pltpu.SemaphoreType.DMA((18,)),
+        ],
+        compiler_params=pltpu.CompilerParams(
+            collective_id=0, has_side_effects=True, vmem_limit_bytes=48 * 1024 * 1024
+        ),
+    )(message, w_gate, w_up, w_down)
+    moe = out.reshape(cols, steps, LANES).transpose(1, 0, 2).reshape(steps, own, width)
+    return moe.astype(jnp.bfloat16), count[0, :steps].reshape(steps, 1)
+
+
 def solution(mesh):
+    dense = mesh.shape["ep"] == 8 and mesh.shape["dp"] == 4
     return jax.shard_map(
-        local,
+        local_gathered if dense else local_packed,
         mesh=mesh,
         in_specs=(
             P(None, ("ep", "dp"), None),

time: 241 us -> 43.4 us (0.18)
  blocking collectives: 74.7 us -> 0 us
  waiting for transfers between devices: 56.6 us -> 0 us
  starting transfers between devices: 51.3 us -> 0 us
  Pallas kernels: 0 us -> 34.5 us
  local copies, waits for them, and re-layouts: 35.8 us -> 5.5 us
  other arithmetic: 13.8 us -> 2.38 us
  matrix products: 5.62 us -> 0 us
    all_gather x12 -> x0, blocking collectives: 62.2 us -> none  [the longest x4 21 us: local(): lax.all_gather(own_slots[step_index], 'dp', axis=0, tiled=True)]
    all_to_all x12 -> x0, waiting for transfers between devices: 56.6 us -> none  [the longest x4 21.5 us: local(): lax.all_to_all(block_out.reshape(ep_count, capacity, model_width), 'ep',...]
    all_to_all x12 -> x0, starting transfers between devices: 51.3 us -> none  [the longest x4 19 us: local(): lax.all_to_all(jnp.repeat(group_counts, 2), 'ep', split_axis=0, concat_ax...]
    pallas_call x0 -> x1, Pallas kernels: none -> 34.5 us  [local_gathered(): pl.pallas_call(functools.partial(moe_kernel, steps), out_shape=(jax.Shape...]
    unnamed x1 -> x0, blocking collectives: 12.6 us -> none
    reshape x28 -> x1, local copies, waits for them, and re-layouts: 7.99 us -> 0.04 us  [local_gathered(): tokens.reshape(steps, cols, LANES).transpose(1, 0, 2)]
    gather x8 -> x0, local copies, waits for them, and re-layouts: 5.66 us -> none  [the longest x4 2.83 us: combine_rows(): paired[:, 0].reshape(-1, model_width)[target].astype(jnp.float32)]
    dot_general x8 -> x0, matrix products: 5.62 us -> none  [the longest x4 3.39 us: expert_block(): jnp.dot(hidden, w_down[0], preferred_element_type=jnp.float32)]
  transfers between devices with their start and end apart: 12 -> 0, of which waited for: 11 -> 0; matrix products, arithmetic and copies ran while one was open for 17% -> 0% of each run, Pallas kernels for 0% -> 0%
where the time goes in v1:
time: 43.4 us; the launch traced here: 43 us
  Pallas kernels  34.5 us (79%)
  local copies, waits for them, and re-layouts  5.5 us (13%)
  other arithmetic  2.38 us (5%)
  between operations  0.68 us (2%)
    pallas_call x1, Pallas kernels, local_gathered(): pl.pallas_call(functools.partial(moe_kernel, steps), out_shape=(jax.Shape...  34.5 us
    unnamed x8, local copies, waits for them, and re-layouts  3.54 us

profile of v1, /device:TPU:0, one launch (start us, length us, event | category | flops | bytes accessed | tf_op | source)
XLA Modules:
  0.0 43.0 jit_solution(11232589101178020331)
XLA Ops:
  0.6 0.0 copy-start.3
  0.6 0.7 %compare_bitcast_fusion = pred[4,2]{0,1:T(4,128)(4,1)S(1)} fusion(s32[4,1,2]{0,2,1:T(2,128)} %param.11), kind=kLoop, calls=%fused_computation.15 | loop fusion | flops 8 | bytes 40 | tf_op jit(solution)/shard_map/eq | solution.py:16
  1.3 0.7 %bitcast_convert_fusion = f32[4,2]{0,1:T(2,128)S(1)} fusion(bf16[4,1,2]{0,2,1:T(2,128)(2,1)} %param.9), kind=kLoop, calls=%fused_computation.16 | loop fusion | flops 8 | bytes 48 | tf_op jit(solution)/shard_map/convert_element_type | solution.py:266
  2.0 0.8 %slice_bitcast_fusion.2 = (s32[4]{0:T(128)S(1)}, s32[4]{0:T(128)S(1)}) fusion(s32[4,2]{0,1:T(2,128)} %param.12), kind=kLoop, calls=%fused_computation.19 | loop fusion | bytes 64 | tf_op jit(solution)/shard_map/squeeze | solution.py:16
  2.7 0.9 %select_reduce_fusion.1 = s32[4,2]{0,1:T(2,128)S(1)} fusion(s32[4]{0:T(128)S(1)} %get-tuple-element.9, s32[4]{0:T(128)S(1)} %get-tuple-element.8, s32[4,2]{0,1:T(2,128)} %bitcast.24, pred[4,2]{0,1:T(4,128)(4,1)S(1)} %compare_bitcast_fusion), kind=kLoop, calls=%fused_computation.13 | loop fusion | flops 120 | bytes 104 | tf_op jit(solution)/shard_map/reduce_sum | solution.py:18
  3.6 0.1 select_reduce_fusion
  3.7 0.1 fusion.5
  3.8 0.0 copy-done.3
  3.9 0.0 copy-start
  3.9 1.2 %copy-done = bf16[1,3584,128]{2,1,0:T(8,128)(2,1)S(1)} copy-done((bf16[1,3584,128]{2,1,0:T(8,128)(2,1)S(1)}, bf16[1,3584,128]{2,1,0:T(8,128)(2,1)}, u32[]{:S(2)}) %copy-start) | copy-done | bytes 917528
  5.0 0.0 copy-start.1
  5.0 1.2 %copy-done.1 = bf16[1,3584,128]{2,1,0:T(8,128)(2,1)S(1)} copy-done((bf16[1,3584,128]{2,1,0:T(8,128)(2,1)S(1)}, bf16[1,3584,128]{2,1,0:T(8,128)(2,1)}, u32[]{:S(2)}) %copy-start.1) | copy-done | bytes 917528
  6.2 0.0 copy-start.2
  6.2 1.2 %copy-done.2 = bf16[1,128,3584]{2,1,0:T(8,128)(2,1)S(1)} copy-done((bf16[1,128,3584]{2,1,0:T(8,128)(2,1)S(1)}, bf16[1,128,3584]{2,1,0:T(8,128)(2,1)}, u32[]{:S(2)}) %copy-start.2) | copy-done | bytes 917528
  7.4 34.5 %shard_map.95 = (f32[112,128]{1,0:T(8,128)S(1)}, s32[1,128]{1,0:T(1,128)S(1)}) custom-call(bf16[128,128]{1,0:T(8,128)(2,1)S(1)} %pad_maximum_fusion.msg_ref, bf16[1,3584,128]{2,1,0:T(8,128)(2,1)S(1)} %copy-done, bf16[1,3584,128]{2,1,0:T(8,128)(2,1)S(1)} %copy-done.1, bf16[1,128,3584]{2,1,0:T(8,128)(2,1)S(1)} %copy-done.2), custom_call_target="tpu_custom_call" | custom-call | tf_op jit(solution)/shard_map/pallas_call | solution.py:277
  41.9 0.5 %slice_bitcast_fusion = s32[4,1]{0,1:T(1,128)} fusion(s32[1,128]{1,0:T(1,128)S(1)} %get-tuple-element.5), kind=kLoop, calls=%fused_computation.17 | loop fusion | bytes 32 | tf_op jit(solution)/shard_map/reshape;squeeze | solution.py:308
  42.4 0.6 %convert_element_type.43 = bf16[4,1,3584]{2,0,1:T(4,128)(2,1)} reshape(bf16[4,28,128]{2,1,0:T(8,128)(2,1)S(1)} %bitcast.20) | data formatting | bytes 57344 | tf_op jit(solution)/shard_map/convert_element_type | solution.py:308
  (5 shorter events, 0.1 us)
Async XLA Ops:
  0.6 3.1 %copy-start.3 = (bf16[4,1,3584]{2,0,1:T(4,128)(2,1)S(1)}, bf16[4,1,3584]{2,0,1:T(4,128)(2,1)}, u32[]{:S(2)}) copy-start(bf16[4,1,3584]{2,0,1:T(4,128)(2,1)} %param.8) | copy-start | bytes 86020
  3.9 1.2 %copy-start = (bf16[1,3584,128]{2,1,0:T(8,128)(2,1)S(1)}, bf16[1,3584,128]{2,1,0:T(8,128)(2,1)}, u32[]{:S(2)}) copy-start(bf16[1,3584,128]{2,1,0:T(8,128)(2,1)} %w_gate_ref.1) | copy-start | bytes 2752516
  5.0 1.2 %copy-start.1 = (bf16[1,3584,128]{2,1,0:T(8,128)(2,1)S(1)}, bf16[1,3584,128]{2,1,0:T(8,128)(2,1)}, u32[]{:S(2)}) copy-start(bf16[1,3584,128]{2,1,0:T(8,128)(2,1)} %w_up_ref.1) | copy-start | bytes 2752516
  6.2 1.2 %copy-start.2 = (bf16[1,128,3584]{2,1,0:T(8,128)(2,1)S(1)}, bf16[1,128,3584]{2,1,0:T(8,128)(2,1)}, u32[]{:S(2)}) copy-start(bf16[1,128,3584]{2,1,0:T(8,128)(2,1)} %w_down_ref.1) | copy-start | bytes 2752516

commit v2 on v0

--- a/solution.py
+++ b/solution.py
@@ -1,7 +1,15 @@
+import functools
+
 import jax
 import jax.numpy as jnp
 from jax import lax
+from jax.experimental import pallas as pl
+from jax.experimental.pallas import tpu as pltpu
 from jax.sharding import PartitionSpec as P
+
+MESH = pl.DeviceIdType.MESH
+LANES = 128
+VMEM_LIMIT = 60 * 1024 * 1024
 
 
 def pick_slots(expert_ids, replica, placement):
@@ -47,7 +55,7 @@
     return jnp.sum(weighted.reshape(row_count, top_count, model_width), axis=1)
 
 
-def local(tokens, route_weight, expert_ids, replica, placement, w_gate, w_up, w_down):
+def local_packed(tokens, route_weight, expert_ids, replica, placement, w_gate, w_up, w_down):
     steps_total = tokens.shape[0]
     model_width = tokens.shape[2]
     ep_count = lax.axis_size("ep")
@@ -92,9 +100,317 @@
     return (jnp.stack(outputs), jnp.stack(load_rows))
 
 
+def moe_kernel(
+    chunks,
+    tok_ref,
+    rw_ref,
+    ids_ref,
+    rep_ref,
+    place_ref,
+    w_gate_ref,
+    w_up_ref,
+    w_down_ref,
+    out_ref,
+    count_ref,
+    rw,
+    ids,
+    rep,
+    place,
+    wgu,
+    wd,
+    extra,
+    zbuf,
+    zextra,
+    gx,
+    ps,
+    cs,
+    cr,
+    first_s,
+    second_s,
+    first_r,
+    second_r,
+    tbuf,
+    zr,
+    wsem,
+    ssem,
+    rsem,
+):
+    ep, dp = lax.axis_index("ep"), lax.axis_index("dp")
+    z, y = ep // 2, ep % 2
+    x, c = dp // 2, dp % 2
+    steps, width = tok_ref.shape
+    hid = w_gate_ref.shape[2]
+    part = width // chunks
+    block = 4 * steps
+    total = 8 * block
+    f32, bf16 = jnp.float32, jnp.bfloat16
+
+    def columns(n, more=0):
+        return pl.ds(n * part, part + more)
+
+    def load(src, dst, n):
+        copy = pltpu.make_async_copy(src, dst, wsem.at[n])
+        copy.start()
+        return copy
+
+    small = [
+        load(src, dst, n)
+        for n, (src, dst) in enumerate(
+            [(rw_ref, rw), (ids_ref, ids), (rep_ref, rep), (place_ref, place)]
+        )
+    ]
+    own = [load(tok_ref.at[:, columns(n)], zbuf.at[n, 0], 4 + n) for n in range(chunks)]
+    weights = [
+        load(w_gate_ref.at[0], wgu.at[:, pl.ds(0, hid)], 4 + chunks),
+        load(w_up_ref.at[0], wgu.at[:, pl.ds(hid, hid)], 5 + chunks),
+        load(w_down_ref.at[0], wd, 6 + chunks),
+    ]
+
+    def device(zz, yy, xx, cc):
+        return (zz * 2 + yy, xx * 2 + cc)
+
+    z_others = [z + 1 - 2 * (z % 2), (z + 2) % 4, 3 - z]
+    z_dev = [device(zz, y, x, c) for zz in z_others]
+    core_dev = device(z, y, x, 1 - c)
+    first_dev = device(z, y + c * (1 - 2 * y), x + (1 - c) * (1 - 2 * x), c)
+    second_dev = device(z, y + (1 - c) * (1 - 2 * y), x + c * (1 - 2 * x), c)
+    slot_a, slot_b = 2 - c, 1 + c
+
+    barrier = pltpu.get_barrier_semaphore()
+    partners = z_dev + [core_dev, first_dev, second_dev]
+    for partner in partners:
+        pl.semaphore_signal(barrier, inc=1, device_id=partner, device_id_type=MESH)
+    pl.semaphore_wait(barrier, len(partners))
+
+    started = []
+
+    def send(src, dst, to):
+        n = len(started)
+        copy = pltpu.make_async_remote_copy(
+            src_ref=src,
+            dst_ref=dst,
+            send_sem=ssem.at[n],
+            recv_sem=rsem.at[n],
+            device_id=to,
+            device_id_type=MESH,
+        )
+        copy.start()
+        started.append(copy)
+        return copy
+
+    z_in = [
+        [send(tok_ref.at[:, columns(n)], zbuf.at[n, k + 1], z_dev[k]) for k in (2, 1, 0)]
+        for n in range(chunks)
+    ]
+
+    for copy in small:
+        copy.wait()
+    lane = lax.broadcasted_iota(jnp.int32, (steps, LANES), 1)
+    diagonal = lax.broadcasted_iota(jnp.int32, (steps, steps), 0) == lax.broadcasted_iota(
+        jnp.int32, (steps, steps), 1
+    )
+    slots = jnp.zeros(ids.shape, jnp.int32)
+    for e in range(place.shape[1]):
+        chosen = jnp.where(rep[...] == 0, place[0:1, e : e + 1], place[1:2, e : e + 1])
+        slots = slots + jnp.where(ids[...] == e, chosen, 0)
+    packed = jnp.zeros((steps, LANES), f32)
+    for k in range(ids.shape[0]):
+        slot = jnp.sum(jnp.where(diagonal, slots[k : k + 1], 0), axis=1, keepdims=True)
+        gain = rw[k : k + 1].astype(f32)
+        gain = jnp.sum(jnp.where(diagonal, gain, 0.0), axis=1, keepdims=True)
+        packed = packed + jnp.where(lane == slot, gain, 0.0)
+        packed = packed + jnp.where(lane == slot + 4, 1.0, 0.0)
+    extra[...] = packed.astype(bf16)
+    z_in.append([send(extra, zextra.at[k + 1], z_dev[k]) for k in (2, 1, 0)])
+
+    def span(n):
+        return columns(n, LANES if n == chunks - 1 else 0)
+
+    first_in, second_in, core_in, diag_in = {}, {}, {}, {}
+
+    def spread(n):
+        own[n].wait()
+        for copy in z_in[n]:
+            copy.wait_recv()
+        gx[0, :, n * part : (n + 1) * part] = jnp.concatenate(
+            [zbuf[n, k] for k in range(4)], axis=0
+        )
+        if n == chunks - 1:
+            for copy in z_in[chunks]:
+                copy.wait_recv()
+            gx[0, :, width : width + LANES] = jnp.concatenate(
+                [extra[...]] + [zextra[k] for k in range(1, 4)], axis=0
+            )
+        here = gx.at[0, :, span(n)]
+        first_in[n] = send(here, gx.at[slot_a, :, span(n)], first_dev)
+        second_in[n] = send(here, gx.at[slot_b, :, span(n)], second_dev)
+        core_in[n] = [send(here, gx.at[4, :, span(n)], core_dev)]
+
+    def forward(n):
+        first_in[n].wait_recv()
+        here = gx.at[slot_a, :, span(n)]
+        diag_in[n] = send(here, gx.at[3, :, span(n)], second_dev)
+        core_in[n].append(send(here, gx.at[4 + slot_a, :, span(n)], core_dev))
+        second_in[n].wait_recv()
+        here = gx.at[slot_b, :, span(n)]
+        core_in[n].append(send(here, gx.at[4 + slot_b, :, span(n)], core_dev))
+
+    def corner(n):
+        diag_in[n].wait_recv()
+        core_in[n].append(send(gx.at[3, :, span(n)], gx.at[7, :, span(n)], core_dev))
+
+    def multiply(n, both):
+        if n == 0:
+            weights[0].wait()
+            weights[1].wait()
+        for copy in core_in[n]:
+            copy.wait_recv()
+        rows = gx[:, :, n * part : (n + 1) * part].reshape(total, part)
+        more = jnp.dot(rows, wgu[n * part : (n + 1) * part], preferred_element_type=f32)
+        return more if both is None else both + more
+
+    both = None
+    for n in range(chunks + 3):
+        if n < chunks:
+            spread(n)
+        if 0 <= n - 1 < chunks:
+            forward(n - 1)
+        if 0 <= n - 2 < chunks:
+            corner(n - 2)
+        if 0 <= n - 3 < chunks:
+            both = multiply(n - 3, both)
+
+    gate, up = both[:, :hid], both[:, hid:]
+    hidden = (gate / (1.0 + jnp.exp(-gate)) * up).astype(bf16)
+    route = gx[:, :, width : width + LANES].reshape(total, LANES).astype(f32)
+    lane = lax.broadcasted_iota(jnp.int32, (total, LANES), 1)
+    weight = jnp.sum(jnp.where(lane == z, route, 0.0), axis=1, keepdims=True)
+    weights[2].wait()
+
+    half = total // 2
+    to_core, diag_out, first_out, second_out, z_out = {}, {}, {}, {}, {}
+
+    def down(n):
+        made = jnp.dot(hidden, wd[:, n * part : (n + 1) * part], preferred_element_type=f32)
+        made = made * weight
+        cs[n] = made[half:].astype(bf16).reshape(4, block, part)
+        to_core[n] = send(cs.at[n], cr.at[n], core_dev)
+        ps[n] = made[:half].reshape(4, block, part)
+
+    def pair(n):
+        to_core[n].wait_recv()
+        first_s[n, 0] = (ps[n, 3] + cr[n, 3].astype(f32)).astype(bf16)
+        diag_out[n] = send(first_s.at[n, 0], first_r.at[n, 0], first_dev)
+        first_s[n, 1] = (ps[n, slot_a] + cr[n, slot_a].astype(f32)).astype(bf16)
+        first_out[n] = send(first_s.at[n, 1], first_r.at[n, 1], first_dev)
+
+    def turn(n):
+        held = ps[n, slot_b] + cr[n, slot_b].astype(f32)
+        diag_out[n].wait_recv()
+        second_s[n] = (held + first_r[n, 0].astype(f32)).astype(bf16)
+        second_out[n] = send(second_s.at[n], second_r.at[n], second_dev)
+
+    def across(n):
+        held = ps[n, 0] + cr[n, 0].astype(f32)
+        first_out[n].wait_recv()
+        held = held + first_r[n, 1].astype(f32)
+        second_out[n].wait_recv()
+        held = (held + second_r[n].astype(f32)).astype(bf16)
+        for k in range(4):
+            tbuf[n, k] = held[k * steps : (k + 1) * steps]
+        z_out[n] = [send(tbuf.at[n, k + 1], zr.at[n, k], z_dev[k]) for k in (2, 1, 0)]
+
+    def finish(n):
+        final = tbuf[n, 0].astype(f32)
+        for copy in z_out[n]:
+            copy.wait_recv()
+        for k in range(3):
+            final = final + zr[n, k].astype(f32)
+        out_ref[:, n * part : (n + 1) * part] = final.astype(out_ref.dtype)
+
+    for n in range(chunks + 4):
+        if n < chunks:
+            down(n)
+        if 0 <= n - 1 < chunks:
+            pair(n - 1)
+        if 0 <= n - 2 < chunks:
+            turn(n - 2)
+        if 0 <= n - 3 < chunks:
+            across(n - 3)
+        if n == chunks:
+            counted = jnp.sum(jnp.where(lane == z + 4, route, 0.0), axis=1, keepdims=True)
+            row = lax.broadcasted_iota(jnp.int32, (total, LANES), 0)
+            per_step = jnp.where(lane == row % steps, counted, 0.0)
+            per_step = jnp.sum(per_step, axis=0, keepdims=True).astype(jnp.int32)
+            count_ref[...] = per_step[:, :steps]
+        if 0 <= n - 4 < chunks:
+            finish(n - 4)
+    for copy in started:
+        copy.wait_send()
+
+
+def local_gathered(tokens, route_weight, expert_ids, replica, placement, w_gate, w_up, w_down):
+    steps, own, width = tokens.shape
+    hid = w_gate.shape[2]
+    top = expert_ids.shape[2]
+    chunks = 4
+    part = width // chunks
+    block = 4 * steps
+    bf16, f32, i32 = jnp.bfloat16, jnp.float32, jnp.int32
+    vmem = pl.BlockSpec(memory_space=pltpu.VMEM)
+    anywhere = pl.BlockSpec(memory_space=pl.ANY)
+    out, count = pl.pallas_call(
+        functools.partial(moe_kernel, chunks),
+        out_shape=(
+            jax.ShapeDtypeStruct((steps, width), bf16),
+            jax.ShapeDtypeStruct((1, steps), i32),
+        ),
+        in_specs=[anywhere] * 8,
+        out_specs=(vmem, vmem),
+        scratch_shapes=[
+            pltpu.VMEM((top, steps), bf16),
+            pltpu.VMEM((top, steps), i32),
+            pltpu.VMEM((top, steps), i32),
+            pltpu.VMEM((2, placement.shape[0]), i32),
+            pltpu.VMEM((width, 2 * hid), bf16),
+            pltpu.VMEM((hid, width), bf16),
+            pltpu.VMEM((steps, LANES), bf16),
+            pltpu.VMEM((chunks, 4, steps, part), bf16),
+            pltpu.VMEM((4, steps, LANES), bf16),
+            pltpu.VMEM((8, block, width + LANES), bf16),
+            pltpu.VMEM((chunks, 4, block, part), f32),
+            pltpu.VMEM((chunks, 4, block, part), bf16),
+            pltpu.VMEM((chunks, 4, block, part), bf16),
+            pltpu.VMEM((chunks, 2, block, part), bf16),
+            pltpu.VMEM((chunks, block, part), bf16),
+            pltpu.VMEM((chunks, 2, block, part), bf16),
+            pltpu.VMEM((chunks, block, part), bf16),
+            pltpu.VMEM((chunks, 4, steps, part), bf16),
+            pltpu.VMEM((chunks, 3, steps, part), bf16),
+            pltpu.SemaphoreType.DMA((7 + chunks,)),
+            pltpu.SemaphoreType.DMA((17 * chunks + 3,)),
+            pltpu.SemaphoreType.DMA((17 * chunks + 3,)),
+        ],
+        compiler_params=pltpu.CompilerParams(
+            collective_id=0, has_side_effects=True, vmem_limit_bytes=VMEM_LIMIT
+        ),
+    )(
+        tokens.reshape(steps, width),
+        route_weight.reshape(steps, top).T,
+        expert_ids.reshape(steps, top).T,
+        replica.reshape(steps, top).T,
+        placement.T,
+        w_gate,
+        w_up,
+        w_down,
+    )
+    return out.reshape(steps, own, width), count.reshape(steps, 1)
+
+
 def solution(mesh):
+    dense = mesh.shape["ep"] == 8 and mesh.shape["dp"] == 4
     return jax.shard_map(
-        local,
+        local_gathered if dense else local_packed,
         mesh=mesh,
         in_specs=(
             P(None, ("ep", "dp"), None),

time: 241 us -> 44 us (0.18)
  blocking collectives: 74.7 us -> 0 us
  waiting for transfers between devices: 56.6 us -> 0 us
  starting transfers between devices: 51.3 us -> 0 us
  Pallas kernels: 0 us -> 41.3 us
  local copies, waits for them, and re-layouts: 35.8 us -> 1.88 us
  other arithmetic: 13.8 us -> 0 us
  matrix products: 5.62 us -> 0 us
    all_gather x12 -> x0, blocking collectives: 62.2 us -> none  [the longest x4 21 us: local(): lax.all_gather(own_slots[step_index], 'dp', axis=0, tiled=True)]
    all_to_all x12 -> x0, waiting for transfers between devices: 56.6 us -> none  [the longest x4 21.5 us: local(): lax.all_to_all(block_out.reshape(ep_count, capacity, model_width), 'ep',...]
    all_to_all x12 -> x0, starting transfers between devices: 51.3 us -> none  [the longest x4 19 us: local(): lax.all_to_all(jnp.repeat(group_counts, 2), 'ep', split_axis=0, concat_ax...]
    pallas_call x0 -> x1, Pallas kernels: none -> 41.3 us  [local_gathered(): pl.pallas_call(functools.partial(moe_kernel, chunks), out_shape=(jax.Shap...]
    unnamed x1 -> x0, blocking collectives: 12.6 us -> none
    reshape x28 -> x0, local copies, waits for them, and re-layouts: 7.99 us -> none  [the longest x4 3.05 us: local(): arrived.reshape(-1, model_width)]
    gather x8 -> x0, local copies, waits for them, and re-layouts: 5.66 us -> none  [the longest x4 2.83 us: combine_rows(): paired[:, 0].reshape(-1, model_width)[target].astype(jnp.float32)]
    dot_general x8 -> x0, matrix products: 5.62 us -> none  [the longest x4 3.39 us: expert_block(): jnp.dot(hidden, w_down[0], preferred_element_type=jnp.float32)]
  transfers between devices with their start and end apart: 12 -> 0, of which waited for: 11 -> 0; matrix products, arithmetic and copies ran while one was open for 17% -> 0% of each run, Pallas kernels for 0% -> 0%
where the time goes in v2:
time: 44 us; the launch traced here: 43.8 us
  Pallas kernels  41.3 us (94%)
  local copies, waits for them, and re-layouts  1.88 us (4%)
  between operations  0.65 us (1%)
    pallas_call x1, Pallas kernels, local_gathered(): pl.pallas_call(functools.partial(moe_kernel, chunks), out_shape=(jax.Shap...  41.3 us
    unnamed x4, local copies, waits for them, and re-layouts  1.88 us

profile of v2, /device:TPU:0, one launch (start us, length us, event | category | flops | bytes accessed | tf_op | source)
XLA Modules:
  0.0 43.8 jit_solution(11375764578477547574)
XLA Ops:
  0.6 41.3 %shard_map.95 = (bf16[4,3584]{1,0:T(4,128)(2,1)}, s32[1,4]{1,0:T(1,128)}) custom-call(bf16[4,3584]{1,0:T(4,128)(2,1)} %bitcast.13, bf16[2,4]{1,0:T(2,128)(2,1)} %bitcast.18, s32[2,4]{1,0:T(2,128)} %bitcast.15, s32[2,4]{1,0:T(2,128)} %bitcast.16, s32[2,4]{1,0:T(2,128)} %bitcast.17, bf16[1,3584,128]{2,1,0:T(8,128)(2,1)} %w_gate_ref.1, ...), custom_call_target="tpu_custom_call" | custom-call | tf_op jit(solution)/shard_map/pallas_call | solution.py:362
  41.9 0.0 copy-start
  41.9 1.4 %copy.12 = bf16[4,1,3584]{2,0,1:T(4,128)(2,1)} copy(bf16[4,1,3584]{2,0,1:T(4,128)(2,1)} %bitcast.14) | data formatting | bytes 57344
  43.3 0.0 copy-done
  43.3 0.5 %copy.13 = s32[4,1]{0,1:T(1,128)} copy(s32[4,1]{0,1:T(1,128)S(1)} %bitcast.19) | data formatting | bytes 32
Async XLA Ops:
  41.9 1.4 %copy-start = (s32[1,4]{1,0:T(1,128)S(1)}, s32[1,4]{1,0:T(1,128)}, u32[]{:S(2)}) copy-start(s32[1,4]{1,0:T(1,128)} %get-tuple-element.5) | copy-start | bytes 52

commit v3 on v2

--- a/solution.py
+++ b/solution.py
@@ -353,7 +353,7 @@
     steps, own, width = tokens.shape
     hid = w_gate.shape[2]
     top = expert_ids.shape[2]
-    chunks = 4
+    chunks = 1
     part = width // chunks
     block = 4 * steps
     bf16, f32, i32 = jnp.bfloat16, jnp.float32, jnp.int32

time: 44 us -> 37.1 us (0.84)
  the two profiles are of different devices: /device:TPU:0 before, /device:TPU:4 now
where the time goes in v3:
time: 37.1 us; the launch traced here: 36.9 us
  Pallas kernels  34.4 us (93%)
  local copies, waits for them, and re-layouts  1.88 us (5%)
  between operations  0.65 us (2%)
    pallas_call x1, Pallas kernels, local_gathered(): pl.pallas_call(functools.partial(moe_kernel, chunks), out_shape=(jax.Shap...  34.4 us
    unnamed x4, local copies, waits for them, and re-layouts  1.88 us

profile of v3, /device:TPU:4, one launch (start us, length us, event | category | flops | bytes accessed | tf_op | source)
XLA Modules:
  0.0 36.9 jit_solution(18444612865358071712)
XLA Ops:
  0.6 34.4 %shard_map.95 = (bf16[4,3584]{1,0:T(4,128)(2,1)}, s32[1,4]{1,0:T(1,128)}) custom-call(bf16[4,3584]{1,0:T(4,128)(2,1)} %bitcast.13, bf16[2,4]{1,0:T(2,128)(2,1)} %bitcast.18, s32[2,4]{1,0:T(2,128)} %bitcast.15, s32[2,4]{1,0:T(2,128)} %bitcast.16, s32[2,4]{1,0:T(2,128)} %bitcast.17, bf16[1,3584,128]{2,1,0:T(8,128)(2,1)} %w_gate_ref.1, ...), custom_call_target="tpu_custom_call" | custom-call | tf_op jit(solution)/shard_map/pallas_call | solution.py:362
  35.0 0.0 copy-start
  35.1 1.4 %copy.12 = bf16[4,1,3584]{2,0,1:T(4,128)(2,1)} copy(bf16[4,1,3584]{2,0,1:T(4,128)(2,1)} %bitcast.14) | data formatting | bytes 57344
  36.4 0.0 copy-done
  36.4 0.5 %copy.13 = s32[4,1]{0,1:T(1,128)} copy(s32[4,1]{0,1:T(1,128)S(1)} %bitcast.19) | data formatting | bytes 32
Async XLA Ops:
  35.0 1.4 %copy-start = (s32[1,4]{1,0:T(1,128)S(1)}, s32[1,4]{1,0:T(1,128)}, u32[]{:S(2)}) copy-start(s32[1,4]{1,0:T(1,128)} %get-tuple-element.5) | copy-start | bytes 52

commit v4 on v3

--- a/solution.py
+++ b/solution.py
@@ -118,17 +118,13 @@
     place,
     wgu,
     wd,
-    extra,
     zbuf,
-    zextra,
     gx,
     ps,
     cs,
     cr,
-    first_s,
-    second_s,
-    first_r,
-    second_r,
+    qs,
+    qr,
     tbuf,
     zr,
     wsem,
@@ -159,7 +155,10 @@
             [(rw_ref, rw), (ids_ref, ids), (rep_ref, rep), (place_ref, place)]
         )
     ]
-    own = [load(tok_ref.at[:, columns(n)], zbuf.at[n, 0], 4 + n) for n in range(chunks)]
+    own = [
+        load(tok_ref.at[:, columns(n)], zbuf.at[n, 0, :, pl.ds(0, part)], 4 + n)
+        for n in range(chunks)
+    ]
     weights = [
         load(w_gate_ref.at[0], wgu.at[:, pl.ds(0, hid)], 4 + chunks),
         load(w_up_ref.at[0], wgu.at[:, pl.ds(hid, hid)], 5 + chunks),
@@ -172,15 +171,15 @@
     z_others = [z + 1 - 2 * (z % 2), (z + 2) % 4, 3 - z]
     z_dev = [device(zz, y, x, c) for zz in z_others]
     core_dev = device(z, y, x, 1 - c)
-    first_dev = device(z, y + c * (1 - 2 * y), x + (1 - c) * (1 - 2 * x), c)
-    second_dev = device(z, y + (1 - c) * (1 - 2 * y), x + c * (1 - 2 * x), c)
-    slot_a, slot_b = 2 - c, 1 + c
+    x_dev = device(z, y, 1 - x, c)
+    y_dev = device(z, 1 - y, x, c)
+    far_dev = device(z, 1 - y, 1 - x, c)
+    plane = [(3, far_dev), (2, x_dev), (1, y_dev)]
 
     barrier = pltpu.get_barrier_semaphore()
-    partners = z_dev + [core_dev, first_dev, second_dev]
+    partners = z_dev + [core_dev, x_dev, y_dev, far_dev]
     for partner in partners:
         pl.semaphore_signal(barrier, inc=1, device_id=partner, device_id_type=MESH)
-    pl.semaphore_wait(barrier, len(partners))
 
     started = []
 
@@ -197,11 +196,6 @@
         copy.start()
         started.append(copy)
         return copy
-
-    z_in = [
-        [send(tok_ref.at[:, columns(n)], zbuf.at[n, k + 1], z_dev[k]) for k in (2, 1, 0)]
-        for n in range(chunks)
-    ]
 
     for copy in small:
         copy.wait()
@@ -220,44 +214,44 @@
         gain = jnp.sum(jnp.where(diagonal, gain, 0.0), axis=1, keepdims=True)
         packed = packed + jnp.where(lane == slot, gain, 0.0)
         packed = packed + jnp.where(lane == slot + 4, 1.0, 0.0)
-    extra[...] = packed.astype(bf16)
-    z_in.append([send(extra, zextra.at[k + 1], z_dev[k]) for k in (2, 1, 0)])
+    zbuf[chunks - 1, 0, :, part:] = packed.astype(bf16)
+    for copy in own:
+        copy.wait()
+    pl.semaphore_wait(barrier, len(partners))
+
+    def wide(n):
+        return pl.ds(0, part + (LANES if n == chunks - 1 else 0))
 
     def span(n):
         return columns(n, LANES if n == chunks - 1 else 0)
 
-    first_in, second_in, core_in, diag_in = {}, {}, {}, {}
+    z_in = [
+        [
+            send(zbuf.at[n, 0, :, wide(n)], zbuf.at[n, k + 1, :, wide(n)], z_dev[k])
+            for k in (2, 1, 0)
+        ]
+        for n in range(chunks)
+    ]
+
+    plane_in, core_in = {}, {}
 
     def spread(n):
-        own[n].wait()
         for copy in z_in[n]:
             copy.wait_recv()
-        gx[0, :, n * part : (n + 1) * part] = jnp.concatenate(
-            [zbuf[n, k] for k in range(4)], axis=0
-        )
-        if n == chunks - 1:
-            for copy in z_in[chunks]:
-                copy.wait_recv()
-            gx[0, :, width : width + LANES] = jnp.concatenate(
-                [extra[...]] + [zextra[k] for k in range(1, 4)], axis=0
-            )
+        end = part + (LANES if n == chunks - 1 else 0)
+        gx[0, :, n * part : n * part + end] = jnp.concatenate(
+            [zbuf[n, k, :, 0:end] for k in range(4)], axis=0
+        )
         here = gx.at[0, :, span(n)]
-        first_in[n] = send(here, gx.at[slot_a, :, span(n)], first_dev)
-        second_in[n] = send(here, gx.at[slot_b, :, span(n)], second_dev)
+        plane_in[n] = [send(here, gx.at[i, :, span(n)], to) for i, to in plane]
         core_in[n] = [send(here, gx.at[4, :, span(n)], core_dev)]
 
     def forward(n):
-        first_in[n].wait_recv()
-        here = gx.at[slot_a, :, span(n)]
-        diag_in[n] = send(here, gx.at[3, :, span(n)], second_dev)
-        core_in[n].append(send(here, gx.at[4 + slot_a, :, span(n)], core_dev))
-        second_in[n].wait_recv()
-        here = gx.at[slot_b, :, span(n)]
-        core_in[n].append(send(here, gx.at[4 + slot_b, :, span(n)], core_dev))
-
-    def corner(n):
-        diag_in[n].wait_recv()
-        core_in[n].append(send(gx.at[3, :, span(n)], gx.at[7, :, span(n)], core_dev))
+        for copy in plane_in[n]:
+            copy.wait_recv()
+        core_in[n].append(
+            send(gx.at[pl.ds(1, 3), :, span(n)], gx.at[pl.ds(5, 3), :, span(n)], core_dev)
+        )
 
     def multiply(n, both):
         if n == 0:
@@ -270,15 +264,13 @@
         return more if both is None else both + more
 
     both = None
-    for n in range(chunks + 3):
+    for n in range(chunks + 2):
         if n < chunks:
             spread(n)
         if 0 <= n - 1 < chunks:
             forward(n - 1)
         if 0 <= n - 2 < chunks:
-            corner(n - 2)
-        if 0 <= n - 3 < chunks:
-            both = multiply(n - 3, both)
+            both = multiply(n - 2, both)
 
     gate, up = both[:, :hid], both[:, hid:]
     hidden = (gate / (1.0 + jnp.exp(-gate)) * up).astype(bf16)
@@ -288,34 +280,29 @@
     weights[2].wait()
 
     half = total // 2
-    to_core, diag_out, first_out, second_out, z_out = {}, {}, {}, {}, {}
+    to_core, plane_out, z_out = {}, {}, {}
 
     def down(n):
-        made = jnp.dot(hidden, wd[:, n * part : (n + 1) * part], preferred_element_type=f32)
-        made = made * weight
-        cs[n] = made[half:].astype(bf16).reshape(4, block, part)
+        held = wd[:, n * part : (n + 1) * part]
+        theirs = jnp.dot(hidden[half:], held, preferred_element_type=f32) * weight[half:]
+        cs[n] = theirs.astype(bf16).reshape(4, block, part)
         to_core[n] = send(cs.at[n], cr.at[n], core_dev)
-        ps[n] = made[:half].reshape(4, block, part)
+        mine = jnp.dot(hidden[:half], held, preferred_element_type=f32) * weight[:half]
+        ps[n] = mine.reshape(4, block, part)
 
     def pair(n):
         to_core[n].wait_recv()
-        first_s[n, 0] = (ps[n, 3] + cr[n, 3].astype(f32)).astype(bf16)
-        diag_out[n] = send(first_s.at[n, 0], first_r.at[n, 0], first_dev)
-        first_s[n, 1] = (ps[n, slot_a] + cr[n, slot_a].astype(f32)).astype(bf16)
-        first_out[n] = send(first_s.at[n, 1], first_r.at[n, 1], first_dev)
-
-    def turn(n):
-        held = ps[n, slot_b] + cr[n, slot_b].astype(f32)
-        diag_out[n].wait_recv()
-        second_s[n] = (held + first_r[n, 0].astype(f32)).astype(bf16)
-        second_out[n] = send(second_s.at[n], second_r.at[n], second_dev)
+        plane_out[n] = []
+        for i, to in plane:
+            qs[n, i - 1] = (ps[n, i] + cr[n, i].astype(f32)).astype(bf16)
+            plane_out[n].append(send(qs.at[n, i - 1], qr.at[n, i - 1], to))
 
     def across(n):
         held = ps[n, 0] + cr[n, 0].astype(f32)
-        first_out[n].wait_recv()
-        held = held + first_r[n, 1].astype(f32)
-        second_out[n].wait_recv()
-        held = (held + second_r[n].astype(f32)).astype(bf16)
+        for (i, _), copy in zip(reversed(plane), reversed(plane_out[n])):
+            copy.wait_recv()
+            held = held + qr[n, i - 1].astype(f32)
+        held = held.astype(bf16)
         for k in range(4):
             tbuf[n, k] = held[k * steps : (k + 1) * steps]
         z_out[n] = [send(tbuf.at[n, k + 1], zr.at[n, k], z_dev[k]) for k in (2, 1, 0)]
@@ -328,23 +315,21 @@
             final = final + zr[n, k].astype(f32)
         out_ref[:, n * part : (n + 1) * part] = final.astype(out_ref.dtype)
 
-    for n in range(chunks + 4):
+    for n in range(chunks + 3):
         if n < chunks:
             down(n)
         if 0 <= n - 1 < chunks:
             pair(n - 1)
         if 0 <= n - 2 < chunks:
-            turn(n - 2)
-        if 0 <= n - 3 < chunks:
-            across(n - 3)
+            across(n - 2)
         if n == chunks:
             counted = jnp.sum(jnp.where(lane == z + 4, route, 0.0), axis=1, keepdims=True)
             row = lax.broadcasted_iota(jnp.int32, (total, LANES), 0)
             per_step = jnp.where(lane == row % steps, counted, 0.0)
             per_step = jnp.sum(per_step, axis=0, keepdims=True).astype(jnp.int32)
             count_ref[...] = per_step[:, :steps]
-        if 0 <= n - 4 < chunks:
-            finish(n - 4)
+        if 0 <= n - 3 < chunks:
+            finish(n - 3)
     for copy in started:
         copy.wait_send()
 
@@ -374,22 +359,18 @@
             pltpu.VMEM((2, placement.shape[0]), i32),
             pltpu.VMEM((width, 2 * hid), bf16),
             pltpu.VMEM((hid, width), bf16),
-            pltpu.VMEM((steps, LANES), bf16),
-            pltpu.VMEM((chunks, 4, steps, part), bf16),
-            pltpu.VMEM((4, steps, LANES), bf16),
+            pltpu.VMEM((chunks, 4, steps, part + LANES), bf16),
             pltpu.VMEM((8, block, width + LANES), bf16),
             pltpu.VMEM((chunks, 4, block, part), f32),
             pltpu.VMEM((chunks, 4, block, part), bf16),
             pltpu.VMEM((chunks, 4, block, part), bf16),
-            pltpu.VMEM((chunks, 2, block, part), bf16),
-            pltpu.VMEM((chunks, block, part), bf16),
-            pltpu.VMEM((chunks, 2, block, part), bf16),
-            pltpu.VMEM((chunks, block, part), bf16),
+            pltpu.VMEM((chunks, 3, block, part), bf16),
+            pltpu.VMEM((chunks, 3, block, part), bf16),
             pltpu.VMEM((chunks, 4, steps, part), bf16),
             pltpu.VMEM((chunks, 3, steps, part), bf16),
             pltpu.SemaphoreType.DMA((7 + chunks,)),
-            pltpu.SemaphoreType.DMA((17 * chunks + 3,)),
-            pltpu.SemaphoreType.DMA((17 * chunks + 3,)),
+            pltpu.SemaphoreType.DMA((15 * chunks,)),
+            pltpu.SemaphoreType.DMA((15 * chunks,)),
         ],
         compiler_params=pltpu.CompilerParams(
             collective_id=0, has_side_effects=True, vmem_limit_bytes=VMEM_LIMIT

time: 37.1 us -> 33.6 us (0.906)
  the two profiles are of different devices: /device:TPU:4 before, /device:TPU:0 now
where the time goes in v4:
time: 33.6 us; the launch traced here: 33.4 us
  Pallas kernels  30.9 us (92%)
  local copies, waits for them, and re-layouts  1.88 us (6%)
  between operations  0.65 us (2%)
    pallas_call x1, Pallas kernels, local_gathered(): pl.pallas_call(functools.partial(moe_kernel, chunks), out_shape=(jax.Shap...  30.9 us
    unnamed x4, local copies, waits for them, and re-layouts  1.88 us

profile of v4, /device:TPU:0, one launch (start us, length us, event | category | flops | bytes accessed | tf_op | source)
XLA Modules:
  0.0 33.4 jit_solution(14379408203192346517)
XLA Ops:
  0.6 30.9 %shard_map.95 = (bf16[4,3584]{1,0:T(4,128)(2,1)}, s32[1,4]{1,0:T(1,128)}) custom-call(bf16[4,3584]{1,0:T(4,128)(2,1)} %bitcast.13, bf16[2,4]{1,0:T(2,128)(2,1)} %bitcast.18, s32[2,4]{1,0:T(2,128)} %bitcast.15, s32[2,4]{1,0:T(2,128)} %bitcast.16, s32[2,4]{1,0:T(2,128)} %bitcast.17, bf16[1,3584,128]{2,1,0:T(8,128)(2,1)} %w_gate_ref.1, ...), custom_call_target="tpu_custom_call" | custom-call | tf_op jit(solution)/shard_map/pallas_call | solution.py:347
  31.5 0.0 copy-start
  31.5 1.4 %copy.12 = bf16[4,1,3584]{2,0,1:T(4,128)(2,1)} copy(bf16[4,1,3584]{2,0,1:T(4,128)(2,1)} %bitcast.14) | data formatting | bytes 57344
  32.9 0.0 copy-done
  32.9 0.5 %copy.13 = s32[4,1]{0,1:T(1,128)} copy(s32[4,1]{0,1:T(1,128)S(1)} %bitcast.19) | data formatting | bytes 32
Async XLA Ops:
  31.5 1.4 %copy-start = (s32[1,4]{1,0:T(1,128)S(1)}, s32[1,4]{1,0:T(1,128)}, u32[]{:S(2)}) copy-start(s32[1,4]{1,0:T(1,128)} %get-tuple-element.5) | copy-start | bytes 52

commit v5 on v4

--- a/solution.py
+++ b/solution.py
@@ -338,7 +338,7 @@
     steps, own, width = tokens.shape
     hid = w_gate.shape[2]
     top = expert_ids.shape[2]
-    chunks = 1
+    chunks = 2
     part = width // chunks
     block = 4 * steps
     bf16, f32, i32 = jnp.bfloat16, jnp.float32, jnp.int32

time: 33.6 us -> 32.5 us (0.967)
  Pallas kernels: 30.9 us -> 29.7 us
    pallas_call x1, Pallas kernels: 30.9 us -> 29.7 us  [local_gathered(): pl.pallas_call(functools.partial(moe_kernel, chunks), out_shape=(jax.Shap...]
where the time goes in v5:
time: 32.5 us; the launch traced here: 32.3 us
  Pallas kernels  29.7 us (91%)
  local copies, waits for them, and re-layouts  1.88 us (6%)
  between operations  0.65 us (2%)
    pallas_call x1, Pallas kernels, local_gathered(): pl.pallas_call(functools.partial(moe_kernel, chunks), out_shape=(jax.Shap...  29.7 us
    unnamed x4, local copies, waits for them, and re-layouts  1.88 us

profile of v5, /device:TPU:0, one launch (start us, length us, event | category | flops | bytes accessed | tf_op | source)
XLA Modules:
  0.0 32.3 jit_solution(8687505404592119813)
XLA Ops:
  0.6 29.7 %shard_map.95 = (bf16[4,3584]{1,0:T(4,128)(2,1)}, s32[1,4]{1,0:T(1,128)}) custom-call(bf16[4,3584]{1,0:T(4,128)(2,1)} %bitcast.13, bf16[2,4]{1,0:T(2,128)(2,1)} %bitcast.18, s32[2,4]{1,0:T(2,128)} %bitcast.15, s32[2,4]{1,0:T(2,128)} %bitcast.16, s32[2,4]{1,0:T(2,128)} %bitcast.17, bf16[1,3584,128]{2,1,0:T(8,128)(2,1)} %w_gate_ref.1, ...), custom_call_target="tpu_custom_call" | custom-call | tf_op jit(solution)/shard_map/pallas_call | solution.py:347
  30.4 0.0 copy-start
  30.4 1.4 %copy.12 = bf16[4,1,3584]{2,0,1:T(4,128)(2,1)} copy(bf16[4,1,3584]{2,0,1:T(4,128)(2,1)} %bitcast.14) | data formatting | bytes 57344
  31.8 0.0 copy-done
  31.8 0.5 %copy.13 = s32[4,1]{0,1:T(1,128)} copy(s32[4,1]{0,1:T(1,128)S(1)} %bitcast.19) | data formatting | bytes 32
Async XLA Ops:
  30.4 1.4 %copy-start = (s32[1,4]{1,0:T(1,128)S(1)}, s32[1,4]{1,0:T(1,128)}, u32[]{:S(2)}) copy-start(s32[1,4]{1,0:T(1,128)} %get-tuple-element.5) | copy-start | bytes 52

commit v6 on v5

--- a/solution.py
+++ b/solution.py
@@ -121,12 +121,12 @@
     zbuf,
     gx,
     ps,
-    cs,
-    cr,
     qs,
     qr,
     tbuf,
     zr,
+    part_count,
+    other_count,
     wsem,
     ssem,
     rsem,
@@ -138,7 +138,7 @@
     hid = w_gate_ref.shape[2]
     part = width // chunks
     block = 4 * steps
-    total = 8 * block
+    total = 4 * block
     f32, bf16 = jnp.float32, jnp.bfloat16
 
     def columns(n, more=0):
@@ -162,7 +162,7 @@
     weights = [
         load(w_gate_ref.at[0], wgu.at[:, pl.ds(0, hid)], 4 + chunks),
         load(w_up_ref.at[0], wgu.at[:, pl.ds(hid, hid)], 5 + chunks),
-        load(w_down_ref.at[0], wd, 6 + chunks),
+        load(w_down_ref.at[0], wd.at[pl.ds(0, hid)], 6 + chunks),
     ]
 
     def device(zz, yy, xx, cc):
@@ -233,7 +233,13 @@
         for n in range(chunks)
     ]
 
-    plane_in, core_in = {}, {}
+    swapped = [
+        send(w_gate_ref.at[0], wgu.at[:, pl.ds(2 * hid, hid)], core_dev),
+        send(w_up_ref.at[0], wgu.at[:, pl.ds(3 * hid, hid)], core_dev),
+        send(w_down_ref.at[0], wd.at[pl.ds(hid, hid)], core_dev),
+    ]
+
+    plane_in = {}
 
     def spread(n):
         for copy in z_in[n]:
@@ -244,61 +250,50 @@
         )
         here = gx.at[0, :, span(n)]
         plane_in[n] = [send(here, gx.at[i, :, span(n)], to) for i, to in plane]
-        core_in[n] = [send(here, gx.at[4, :, span(n)], core_dev)]
-
-    def forward(n):
-        for copy in plane_in[n]:
-            copy.wait_recv()
-        core_in[n].append(
-            send(gx.at[pl.ds(1, 3), :, span(n)], gx.at[pl.ds(5, 3), :, span(n)], core_dev)
-        )
 
     def multiply(n, both):
         if n == 0:
             weights[0].wait()
             weights[1].wait()
-        for copy in core_in[n]:
+            swapped[0].wait_recv()
+            swapped[1].wait_recv()
+        for copy in plane_in[n]:
             copy.wait_recv()
         rows = gx[:, :, n * part : (n + 1) * part].reshape(total, part)
         more = jnp.dot(rows, wgu[n * part : (n + 1) * part], preferred_element_type=f32)
         return more if both is None else both + more
 
     both = None
-    for n in range(chunks + 2):
-        if n < chunks:
-            spread(n)
-        if 0 <= n - 1 < chunks:
-            forward(n - 1)
-        if 0 <= n - 2 < chunks:
-            both = multiply(n - 2, both)
-
-    gate, up = both[:, :hid], both[:, hid:]
-    hidden = (gate / (1.0 + jnp.exp(-gate)) * up).astype(bf16)
+    for n in range(chunks):
+        spread(n)
+    for n in range(chunks):
+        both = multiply(n, both)
+
+    hidden = []
+    for i in range(2):
+        gate, up = both[:, 2 * i * hid : (2 * i + 1) * hid], both[:, (2 * i + 1) * hid : (2 * i + 2) * hid]
+        hidden.append((gate / (1.0 + jnp.exp(-gate)) * up).astype(bf16))
+    hidden = jnp.concatenate(hidden, axis=1)
     route = gx[:, :, width : width + LANES].reshape(total, LANES).astype(f32)
     lane = lax.broadcasted_iota(jnp.int32, (total, LANES), 1)
     weight = jnp.sum(jnp.where(lane == z, route, 0.0), axis=1, keepdims=True)
     weights[2].wait()
-
-    half = total // 2
-    to_core, plane_out, z_out = {}, {}, {}
+    swapped[2].wait_recv()
+
+    plane_out, z_out = {}, {}
 
     def down(n):
         held = wd[:, n * part : (n + 1) * part]
-        theirs = jnp.dot(hidden[half:], held, preferred_element_type=f32) * weight[half:]
-        cs[n] = theirs.astype(bf16).reshape(4, block, part)
-        to_core[n] = send(cs.at[n], cr.at[n], core_dev)
-        mine = jnp.dot(hidden[:half], held, preferred_element_type=f32) * weight[:half]
-        ps[n] = mine.reshape(4, block, part)
-
-    def pair(n):
-        to_core[n].wait_recv()
+        made = jnp.dot(hidden, held, preferred_element_type=f32) * weight
+        made = made.reshape(4, block, part)
         plane_out[n] = []
         for i, to in plane:
-            qs[n, i - 1] = (ps[n, i] + cr[n, i].astype(f32)).astype(bf16)
+            qs[n, i - 1] = made[i].astype(bf16)
             plane_out[n].append(send(qs.at[n, i - 1], qr.at[n, i - 1], to))
+        ps[n] = made[0]
 
     def across(n):
-        held = ps[n, 0] + cr[n, 0].astype(f32)
+        held = ps[n]
         for (i, _), copy in zip(reversed(plane), reversed(plane_out[n])):
             copy.wait_recv()
             held = held + qr[n, i - 1].astype(f32)
@@ -315,21 +310,20 @@
             final = final + zr[n, k].astype(f32)
         out_ref[:, n * part : (n + 1) * part] = final.astype(out_ref.dtype)
 
-    for n in range(chunks + 3):
-        if n < chunks:
-            down(n)
-        if 0 <= n - 1 < chunks:
-            pair(n - 1)
-        if 0 <= n - 2 < chunks:
-            across(n - 2)
-        if n == chunks:
-            counted = jnp.sum(jnp.where(lane == z + 4, route, 0.0), axis=1, keepdims=True)
-            row = lax.broadcasted_iota(jnp.int32, (total, LANES), 0)
-            per_step = jnp.where(lane == row % steps, counted, 0.0)
-            per_step = jnp.sum(per_step, axis=0, keepdims=True).astype(jnp.int32)
-            count_ref[...] = per_step[:, :steps]
-        if 0 <= n - 3 < chunks:
-            finish(n - 3)
+    for n in range(chunks):
+        down(n)
+    counted = jnp.sum(jnp.where(lane == z + 4, route, 0.0), axis=1, keepdims=True)
+    row = lax.broadcasted_iota(jnp.int32, (total, LANES), 0)
+    per_step = jnp.where(lane == row % steps, counted, 0.0)
+    per_step = jnp.sum(per_step, axis=0, keepdims=True)
+    part_count[...] = jnp.broadcast_to(per_step, part_count.shape)
+    count_in = send(part_count, other_count, core_dev)
+    for n in range(chunks):
+        across(n)
+    count_in.wait_recv()
+    count_ref[...] = (part_count[...] + other_count[...])[0:1, :steps].astype(jnp.int32)
+    for n in range(chunks):
+        finish(n)
     for copy in started:
         copy.wait_send()
 
@@ -357,20 +351,20 @@
             pltpu.VMEM((top, steps), i32),
             pltpu.VMEM((top, steps), i32),
             pltpu.VMEM((2, placement.shape[0]), i32),
-            pltpu.VMEM((width, 2 * hid), bf16),
-            pltpu.VMEM((hid, width), bf16),
+            pltpu.VMEM((width, 4 * hid), bf16),
+            pltpu.VMEM((2 * hid, width), bf16),
             pltpu.VMEM((chunks, 4, steps, part + LANES), bf16),
-            pltpu.VMEM((8, block, width + LANES), bf16),
-            pltpu.VMEM((chunks, 4, block, part), f32),
-            pltpu.VMEM((chunks, 4, block, part), bf16),
-            pltpu.VMEM((chunks, 4, block, part), bf16),
+            pltpu.VMEM((4, block, width + LANES), bf16),
+            pltpu.VMEM((chunks, block, part), f32),
             pltpu.VMEM((chunks, 3, block, part), bf16),
             pltpu.VMEM((chunks, 3, block, part), bf16),
             pltpu.VMEM((chunks, 4, steps, part), bf16),
             pltpu.VMEM((chunks, 3, steps, part), bf16),
+            pltpu.VMEM((8, LANES), f32),
+            pltpu.VMEM((8, LANES), f32),
             pltpu.SemaphoreType.DMA((7 + chunks,)),
-            pltpu.SemaphoreType.DMA((15 * chunks,)),
-            pltpu.SemaphoreType.DMA((15 * chunks,)),
+            pltpu.SemaphoreType.DMA((12 * chunks + 4,)),
+            pltpu.SemaphoreType.DMA((12 * chunks + 4,)),
         ],
         compiler_params=pltpu.CompilerParams(
             collective_id=0, has_side_effects=True, vmem_limit_bytes=VMEM_LIMIT

time: 32.5 us -> 29.4 us (0.905)
  Pallas kernels: 29.7 us -> 26.7 us
    pallas_call x1, Pallas kernels: 29.7 us -> 26.7 us  [local_gathered(): pl.pallas_call(functools.partial(moe_kernel, chunks), out_shape=(jax.Shap...]
where the time goes in v6:
time: 29.4 us; the launch traced here: 29.2 us
  Pallas kernels  26.7 us (91%)
  local copies, waits for them, and re-layouts  1.88 us (6%)
  between operations  0.65 us (2%)
    pallas_call x1, Pallas kernels, local_gathered(): pl.pallas_call(functools.partial(moe_kernel, chunks), out_shape=(jax.Shap...  26.7 us
    unnamed x4, local copies, waits for them, and re-layouts  1.88 us

profile of v6, /device:TPU:0, one launch (start us, length us, event | category | flops | bytes accessed | tf_op | source)
XLA Modules:
  0.0 29.2 jit_solution(13426510325091252642)
XLA Ops:
  0.6 26.7 %shard_map.95 = (bf16[4,3584]{1,0:T(4,128)(2,1)}, s32[1,4]{1,0:T(1,128)}) custom-call(bf16[4,3584]{1,0:T(4,128)(2,1)} %bitcast.13, bf16[2,4]{1,0:T(2,128)(2,1)} %bitcast.18, s32[2,4]{1,0:T(2,128)} %bitcast.15, s32[2,4]{1,0:T(2,128)} %bitcast.16, s32[2,4]{1,0:T(2,128)} %bitcast.17, bf16[1,3584,128]{2,1,0:T(8,128)(2,1)} %w_gate_ref.1, ...), custom_call_target="tpu_custom_call" | custom-call | tf_op jit(solution)/shard_map/pallas_call | solution.py:341
  27.3 0.0 copy-start
  27.3 1.4 %copy.12 = bf16[4,1,3584]{2,0,1:T(4,128)(2,1)} copy(bf16[4,1,3584]{2,0,1:T(4,128)(2,1)} %bitcast.14) | data formatting | bytes 57344
  28.7 0.0 copy-done
  28.7 0.5 %copy.13 = s32[4,1]{0,1:T(1,128)} copy(s32[4,1]{0,1:T(1,128)S(1)} %bitcast.19) | data formatting | bytes 32
Async XLA Ops:
  27.3 1.4 %copy-start = (s32[1,4]{1,0:T(1,128)S(1)}, s32[1,4]{1,0:T(1,128)}, u32[]{:S(2)}) copy-start(s32[1,4]{1,0:T(1,128)} %get-tuple-element.5) | copy-start | bytes 52

commit v7 on v6

--- a/solution.py
+++ b/solution.py
@@ -326,6 +326,17 @@
         finish(n)
     for copy in started:
         copy.wait_send()
+
+
+def hand_over(made_ref, made_count_ref, out_ref, count_ref, sem):
+    copies = [
+        pltpu.make_async_copy(made_ref, out_ref, sem.at[0]),
+        pltpu.make_async_copy(made_count_ref, count_ref, sem.at[1]),
+    ]
+    for copy in copies:
+        copy.start()
+    for copy in copies:
+        copy.wait()
 
 
 def local_gathered(tokens, route_weight, expert_ids, replica, placement, w_gate, w_up, w_down):
@@ -379,6 +390,17 @@
         w_up,
         w_down,
     )
+    out, count = pl.pallas_call(
+        hand_over,
+        out_shape=(
+            jax.ShapeDtypeStruct(out.shape, out.dtype),
+            jax.ShapeDtypeStruct(count.shape, count.dtype),
+        ),
+        in_specs=[anywhere] * 2,
+        out_specs=(anywhere, anywhere),
+        scratch_shapes=[pltpu.SemaphoreType.DMA((2,))],
+        compiler_params=pltpu.CompilerParams(vmem_limit_bytes=VMEM_LIMIT),
+    )(out, count)
     return out.reshape(steps, own, width), count.reshape(steps, 1)
 
 

time: 29.4 us -> 29.5 us (level)
  Pallas kernels: 26.7 us -> 28.7 us
  local copies, waits for them, and re-layouts: 1.88 us -> 0 us
    pallas_call x0 -> x1, Pallas kernels: none -> 2.01 us  [local_gathered(): pl.pallas_call(hand_over, out_shape=(jax.ShapeDtypeStruct(out.shape, out....]
    unnamed x4 -> x0, local copies, waits for them, and re-layouts: 1.88 us -> none
where the time goes in v7:
time: 29.5 us; the launch traced here: 29.3 us
  Pallas kernels  28.7 us (97%)
  between operations  0.64 us (2%)
    pallas_call x1, Pallas kernels, local_gathered(): pl.pallas_call(functools.partial(moe_kernel, chunks), out_shape=(jax.Shap...  26.7 us
    pallas_call x1, Pallas kernels, local_gathered(): pl.pallas_call(hand_over, out_shape=(jax.ShapeDtypeStruct(out.shape, out....  2.01 us

profile of v7, /device:TPU:0, one launch (start us, length us, event | category | flops | bytes accessed | tf_op | source)
XLA Modules:
  0.0 29.3 jit_solution(9514828689719499524)
XLA Ops:
  0.6 26.7 %shard_map.95 = (bf16[4,3584]{1,0:T(4,128)(2,1)}, s32[1,4]{1,0:T(1,128)}) custom-call(bf16[4,3584]{1,0:T(4,128)(2,1)} %bitcast.13, bf16[2,4]{1,0:T(2,128)(2,1)} %bitcast.17, s32[2,4]{1,0:T(2,128)} %bitcast.14, s32[2,4]{1,0:T(2,128)} %bitcast.15, s32[2,4]{1,0:T(2,128)} %bitcast.16, bf16[1,3584,128]{2,1,0:T(8,128)(2,1)} %w_gate_ref.1, ...), custom_call_target="tpu_custom_call" | custom-call | tf_op jit(solution)/shard_map/pallas_call | solution.py:352
  27.3 2.0 %shard_map.96 = (bf16[4,3584]{1,0:T(4,128)(2,1)}, s32[1,4]{1,0:T(1,128)}) custom-call(bf16[4,3584]{1,0:T(4,128)(2,1)} %get-tuple-element.6.made_ref, s32[1,4]{1,0:T(1,128)} %get-tuple-element.7.made_count_ref), custom_call_target="tpu_custom_call" | custom-call | tf_op jit(solution)/shard_map/pallas_call | solution.py:393

commit v8 on v6

--- a/solution.py
+++ b/solution.py
@@ -101,7 +101,7 @@
 
 
 def moe_kernel(
-    chunks,
+    tiles,
     tok_ref,
     rw_ref,
     ids_ref,
@@ -136,13 +136,18 @@
     x, c = dp // 2, dp % 2
     steps, width = tok_ref.shape
     hid = w_gate_ref.shape[2]
-    part = width // chunks
+    chunks = len(tiles)
+    edges = [sum(tiles[:n]) * LANES for n in range(chunks + 1)]
+    ends = edges[1:chunks] + [width + LANES]
     block = 4 * steps
     total = 4 * block
     f32, bf16 = jnp.float32, jnp.bfloat16
 
-    def columns(n, more=0):
-        return pl.ds(n * part, part + more)
+    def columns(n):
+        return pl.ds(edges[n], edges[n + 1] - edges[n])
+
+    def span(n):
+        return pl.ds(edges[n], ends[n] - edges[n])
 
     def load(src, dst, n):
         copy = pltpu.make_async_copy(src, dst, wsem.at[n])
@@ -156,7 +161,7 @@
         )
     ]
     own = [
-        load(tok_ref.at[:, columns(n)], zbuf.at[n, 0, :, pl.ds(0, part)], 4 + n)
+        load(tok_ref.at[:, columns(n)], zbuf.at[0, :, columns(n)], 4 + n)
         for n in range(chunks)
     ]
     weights = [
@@ -214,20 +219,14 @@
         gain = jnp.sum(jnp.where(diagonal, gain, 0.0), axis=1, keepdims=True)
         packed = packed + jnp.where(lane == slot, gain, 0.0)
         packed = packed + jnp.where(lane == slot + 4, 1.0, 0.0)
-    zbuf[chunks - 1, 0, :, part:] = packed.astype(bf16)
+    zbuf[0, :, width:] = packed.astype(bf16)
     for copy in own:
         copy.wait()
     pl.semaphore_wait(barrier, len(partners))
 
-    def wide(n):
-        return pl.ds(0, part + (LANES if n == chunks - 1 else 0))
-
-    def span(n):
-        return columns(n, LANES if n == chunks - 1 else 0)
-
     z_in = [
         [
-            send(zbuf.at[n, 0, :, wide(n)], zbuf.at[n, k + 1, :, wide(n)], z_dev[k])
+            send(zbuf.at[0, :, span(n)], zbuf.at[k + 1, :, span(n)], z_dev[k])
             for k in (2, 1, 0)
         ]
         for n in range(chunks)
@@ -244,10 +243,8 @@
     def spread(n):
         for copy in z_in[n]:
             copy.wait_recv()
-        end = part + (LANES if n == chunks - 1 else 0)
-        gx[0, :, n * part : n * part + end] = jnp.concatenate(
-            [zbuf[n, k, :, 0:end] for k in range(4)], axis=0
-        )
+        lo, hi = edges[n], ends[n]
+        gx[0, :, lo:hi] = jnp.concatenate([zbuf[k, :, lo:hi] for k in range(4)], axis=0)
         here = gx.at[0, :, span(n)]
         plane_in[n] = [send(here, gx.at[i, :, span(n)], to) for i, to in plane]
 
@@ -259,8 +256,9 @@
             swapped[1].wait_recv()
         for copy in plane_in[n]:
             copy.wait_recv()
-        rows = gx[:, :, n * part : (n + 1) * part].reshape(total, part)
-        more = jnp.dot(rows, wgu[n * part : (n + 1) * part], preferred_element_type=f32)
+        lo, hi = edges[n], edges[n + 1]
+        rows = gx[:, :, lo:hi].reshape(total, hi - lo)
+        more = jnp.dot(rows, wgu[lo:hi], preferred_element_type=f32)
         return more if both is None else both + more
 
     both = None
@@ -283,32 +281,38 @@
     plane_out, z_out = {}, {}
 
     def down(n):
-        held = wd[:, n * part : (n + 1) * part]
-        made = jnp.dot(hidden, held, preferred_element_type=f32) * weight
-        made = made.reshape(4, block, part)
+        lo, hi = edges[n], edges[n + 1]
+        made = jnp.dot(hidden, wd[:, lo:hi], preferred_element_type=f32) * weight
+        made = made.reshape(4, block, hi - lo)
         plane_out[n] = []
         for i, to in plane:
-            qs[n, i - 1] = made[i].astype(bf16)
-            plane_out[n].append(send(qs.at[n, i - 1], qr.at[n, i - 1], to))
-        ps[n] = made[0]
+            qs[i - 1, :, lo:hi] = made[i].astype(bf16)
+            here = qs.at[i - 1, :, columns(n)]
+            plane_out[n].append(send(here, qr.at[i - 1, :, columns(n)], to))
+        ps[:, lo:hi] = made[0]
 
     def across(n):
-        held = ps[n]
+        lo, hi = edges[n], edges[n + 1]
+        held = ps[:, lo:hi]
         for (i, _), copy in zip(reversed(plane), reversed(plane_out[n])):
             copy.wait_recv()
-            held = held + qr[n, i - 1].astype(f32)
+            held = held + qr[i - 1, :, lo:hi].astype(f32)
         held = held.astype(bf16)
         for k in range(4):
-            tbuf[n, k] = held[k * steps : (k + 1) * steps]
-        z_out[n] = [send(tbuf.at[n, k + 1], zr.at[n, k], z_dev[k]) for k in (2, 1, 0)]
+            tbuf[k, :, lo:hi] = held[k * steps : (k + 1) * steps]
+        z_out[n] = [
+            send(tbuf.at[k + 1, :, columns(n)], zr.at[k, :, columns(n)], z_dev[k])
+            for k in (2, 1, 0)
+        ]
 
     def finish(n):
-        final = tbuf[n, 0].astype(f32)
+        lo, hi = edges[n], edges[n + 1]
+        final = tbuf[0, :, lo:hi].astype(f32)
         for copy in z_out[n]:
             copy.wait_recv()
         for k in range(3):
-            final = final + zr[n, k].astype(f32)
-        out_ref[:, n * part : (n + 1) * part] = final.astype(out_ref.dtype)
+            final = final + zr[k, :, lo:hi].astype(f32)
+        out_ref[:, lo:hi] = final.astype(out_ref.dtype)
 
     for n in range(chunks):
         down(n)
@@ -332,16 +336,17 @@
     steps, own, width = tokens.shape
     hid = w_gate.shape[2]
     top = expert_ids.shape[2]
-    chunks = 2
-    part = width // chunks
+    cols = width // LANES
+    tiles = [2 * cols // 7, cols - 2 * (2 * cols // 7), 2 * cols // 7]
+    chunks = len(tiles)
     block = 4 * steps
     bf16, f32, i32 = jnp.bfloat16, jnp.float32, jnp.int32
     vmem = pl.BlockSpec(memory_space=pltpu.VMEM)
     anywhere = pl.BlockSpec(memory_space=pl.ANY)
     out, count = pl.pallas_call(
-        functools.partial(moe_kernel, chunks),
+        functools.partial(moe_kernel, tiles),
         out_shape=(
-            jax.ShapeDtypeStruct((steps, width), bf16),
+            jax.ShapeDtypeStruct((steps, width), f32),
             jax.ShapeDtypeStruct((1, steps), i32),
         ),
         in_specs=[anywhere] * 8,
@@ -353,13 +358,13 @@
             pltpu.VMEM((2, placement.shape[0]), i32),
             pltpu.VMEM((width, 4 * hid), bf16),
             pltpu.VMEM((2 * hid, width), bf16),
-            pltpu.VMEM((chunks, 4, steps, part + LANES), bf16),
+            pltpu.VMEM((4, steps, width + LANES), bf16),
             pltpu.VMEM((4, block, width + LANES), bf16),
-            pltpu.VMEM((chunks, block, part), f32),
-            pltpu.VMEM((chunks, 3, block, part), bf16),
-            pltpu.VMEM((chunks, 3, block, part), bf16),
-            pltpu.VMEM((chunks, 4, steps, part), bf16),
-            pltpu.VMEM((chunks, 3, steps, part), bf16),
+            pltpu.VMEM((block, width), f32),
+            pltpu.VMEM((3, block, width), bf16),
+            pltpu.VMEM((3, block, width), bf16),
+            pltpu.VMEM((4, steps, width), bf16),
+            pltpu.VMEM((3, steps, width), bf16),
             pltpu.VMEM((8, LANES), f32),
             pltpu.VMEM((8, LANES), f32),
             pltpu.SemaphoreType.DMA((7 + chunks,)),
@@ -379,7 +384,7 @@
         w_up,
         w_down,
     )
-    return out.reshape(steps, own, width), count.reshape(steps, 1)
+    return out.astype(bf16).reshape(steps, own, width), count.reshape(steps, 1)
 
 
 def solution(mesh):

time: 29.4 us -> 29.2 us (level)
  other arithmetic: 0 us -> 1.44 us
  Pallas kernels: 26.7 us -> 25.8 us
  local copies, waits for them, and re-layouts: 1.88 us -> 1.11 us
    reshape x0 -> x1, other arithmetic: none -> 1.44 us  [local_gathered(): out.astype(bf16).reshape(steps, own, width)]
    pallas_call x1, Pallas kernels: 26.7 us -> 25.8 us  [local_gathered(): pl.pallas_call(functools.partial(moe_kernel, tiles), out_shape=(jax.Shape...]
    unnamed x4 -> x3, local copies, waits for them, and re-layouts: 1.88 us -> 1.11 us
where the time goes in v8:
time: 29.2 us; the launch traced here: 29 us
  Pallas kernels  25.8 us (88%)
  other arithmetic  1.44 us (5%)
  local copies, waits for them, and re-layouts  1.11 us (4%)
  between operations  0.64 us (2%)
    pallas_call x1, Pallas kernels, local_gathered(): pl.pallas_call(functools.partial(moe_kernel, tiles), out_shape=(jax.Shape...  25.8 us
    reshape x1, other arithmetic, local_gathered(): out.astype(bf16).reshape(steps, own, width)  1.44 us
    unnamed x3, local copies, waits for them, and re-layouts  1.11 us

profile of v8, /device:TPU:0, one launch (start us, length us, event | category | flops | bytes accessed | tf_op | source)
XLA Modules:
  0.0 29.0 jit_solution(6071624653497165234)
XLA Ops:
  0.6 25.8 %shard_map.95 = (f32[4,3584]{1,0:T(4,128)}, s32[1,4]{1,0:T(1,128)}) custom-call(bf16[4,3584]{1,0:T(4,128)(2,1)} %bitcast.14, bf16[2,4]{1,0:T(2,128)(2,1)} %bitcast.18, s32[2,4]{1,0:T(2,128)} %bitcast.15, s32[2,4]{1,0:T(2,128)} %bitcast.16, s32[2,4]{1,0:T(2,128)} %bitcast.17, bf16[1,3584,128]{2,1,0:T(8,128)(2,1)} %w_gate_ref.1, ...), custom_call_target="tpu_custom_call" | custom-call | tf_op jit(solution)/shard_map/pallas_call | solution.py:346
  26.5 1.4 %convert_bitcast_fusion = bf16[4,1,3584]{2,0,1:T(4,128)(2,1)} fusion(f32[4,3584]{1,0:T(4,128)} %get-tuple-element.4), kind=kLoop, calls=%fused_computation | loop fusion | flops 14336 | bytes 86016 | tf_op jit(solution)/shard_map/reshape | solution.py:387
  27.9 0.0 copy-start
  27.9 0.6 %copy-done = s32[1,4]{1,0:T(1,128)S(1)} copy-done((s32[1,4]{1,0:T(1,128)S(1)}, s32[1,4]{1,0:T(1,128)}, u32[]{:S(2)}) %copy-start) | copy-done | bytes 40
  28.5 0.5 %copy.11 = s32[4,1]{0,1:T(1,128)} copy(s32[4,1]{0,1:T(1,128)S(1)} %bitcast.19) | data formatting | bytes 32
Async XLA Ops:
  27.9 0.6 %copy-start = (s32[1,4]{1,0:T(1,128)S(1)}, s32[1,4]{1,0:T(1,128)}, u32[]{:S(2)}) copy-start(s32[1,4]{1,0:T(1,128)} %get-tuple-element.5) | copy-start | bytes 52

commit v9 on v8

--- a/solution.py
+++ b/solution.py
@@ -346,7 +346,7 @@
     out, count = pl.pallas_call(
         functools.partial(moe_kernel, tiles),
         out_shape=(
-            jax.ShapeDtypeStruct((steps, width), f32),
+            jax.ShapeDtypeStruct((steps, width), bf16),
             jax.ShapeDtypeStruct((1, steps), i32),
         ),
         in_specs=[anywhere] * 8,
@@ -384,7 +384,7 @@
         w_up,
         w_down,
     )
-    return out.astype(bf16).reshape(steps, own, width), count.reshape(steps, 1)
+    return out.reshape(steps, own, width), count.reshape(steps, 1)
 
 
 def solution(mesh):

time: 29.2 us -> 28.5 us (0.976)
  other arithmetic: 1.44 us -> 0 us
  local copies, waits for them, and re-layouts: 1.11 us -> 1.88 us
    reshape x1 -> x0, other arithmetic: 1.44 us -> none  [local_gathered(): out.astype(bf16).reshape(steps, own, width)]
    unnamed x3 -> x4, local copies, waits for them, and re-layouts: 1.11 us -> 1.88 us
where the time goes in v9:
time: 28.5 us; the launch traced here: 28.4 us
  Pallas kernels  25.8 us (91%)
  local copies, waits for them, and re-layouts  1.88 us (7%)
  between operations  0.65 us (2%)
    pallas_call x1, Pallas kernels, local_gathered(): pl.pallas_call(functools.partial(moe_kernel, tiles), out_shape=(jax.Shape...  25.8 us
    unnamed x4, local copies, waits for them, and re-layouts  1.88 us

profile of v9, /device:TPU:0, one launch (start us, length us, event | category | flops | bytes accessed | tf_op | source)
XLA Modules:
  0.0 28.4 jit_solution(3339318162329887481)
XLA Ops:
  0.6 25.8 %shard_map.95 = (bf16[4,3584]{1,0:T(4,128)(2,1)}, s32[1,4]{1,0:T(1,128)}) custom-call(bf16[4,3584]{1,0:T(4,128)(2,1)} %bitcast.13, bf16[2,4]{1,0:T(2,128)(2,1)} %bitcast.18, s32[2,4]{1,0:T(2,128)} %bitcast.15, s32[2,4]{1,0:T(2,128)} %bitcast.16, s32[2,4]{1,0:T(2,128)} %bitcast.17, bf16[1,3584,128]{2,1,0:T(8,128)(2,1)} %w_gate_ref.1, ...), custom_call_target="tpu_custom_call" | custom-call | tf_op jit(solution)/shard_map/pallas_call | solution.py:346
  26.5 0.0 copy-start
  26.5 1.4 %copy.12 = bf16[4,1,3584]{2,0,1:T(4,128)(2,1)} copy(bf16[4,1,3584]{2,0,1:T(4,128)(2,1)} %bitcast.14) | data formatting | bytes 57344
  27.8 0.0 copy-done
  27.8 0.5 %copy.13 = s32[4,1]{0,1:T(1,128)} copy(s32[4,1]{0,1:T(1,128)S(1)} %bitcast.19) | data formatting | bytes 32
Async XLA Ops:
  26.5 1.4 %copy-start = (s32[1,4]{1,0:T(1,128)S(1)}, s32[1,4]{1,0:T(1,128)}, u32[]{:S(2)}) copy-start(s32[1,4]{1,0:T(1,128)} %get-tuple-element.5) | copy-start | bytes 52

commit v10 on v9

--- a/solution.py
+++ b/solution.py
@@ -179,7 +179,7 @@
     x_dev = device(z, y, 1 - x, c)
     y_dev = device(z, 1 - y, x, c)
     far_dev = device(z, 1 - y, 1 - x, c)
-    plane = [(3, far_dev), (2, x_dev), (1, y_dev)]
+    plane = [(1, y_dev), (3, far_dev), (2, x_dev)]
 
     barrier = pltpu.get_barrier_semaphore()
     partners = z_dev + [core_dev, x_dev, y_dev, far_dev]

time: 28.5 us -> 28.6 us (level)
  no operation moved by 1% of the time
where the time goes in v10:
time: 28.6 us; the launch traced here: 28.4 us
  Pallas kernels  25.8 us (90%)
  local copies, waits for them, and re-layouts  1.88 us (7%)
  between operations  0.65 us (2%)
    pallas_call x1, Pallas kernels, local_gathered(): pl.pallas_call(functools.partial(moe_kernel, tiles), out_shape=(jax.Shape...  25.8 us
    unnamed x4, local copies, waits for them, and re-layouts  1.88 us

profile of v10, /device:TPU:0, one launch (start us, length us, event | category | flops | bytes accessed | tf_op | source)
XLA Modules:
  0.0 28.4 jit_solution(13784946191461044068)
XLA Ops:
  0.6 25.8 %shard_map.95 = (bf16[4,3584]{1,0:T(4,128)(2,1)}, s32[1,4]{1,0:T(1,128)}) custom-call(bf16[4,3584]{1,0:T(4,128)(2,1)} %bitcast.13, bf16[2,4]{1,0:T(2,128)(2,1)} %bitcast.18, s32[2,4]{1,0:T(2,128)} %bitcast.15, s32[2,4]{1,0:T(2,128)} %bitcast.16, s32[2,4]{1,0:T(2,128)} %bitcast.17, bf16[1,3584,128]{2,1,0:T(8,128)(2,1)} %w_gate_ref.1, ...), custom_call_target="tpu_custom_call" | custom-call | tf_op jit(solution)/shard_map/pallas_call | solution.py:346
  26.5 0.0 copy-start
  26.5 1.4 %copy.12 = bf16[4,1,3584]{2,0,1:T(4,128)(2,1)} copy(bf16[4,1,3584]{2,0,1:T(4,128)(2,1)} %bitcast.14) | data formatting | bytes 57344
  27.8 0.0 copy-done
  27.8 0.5 %copy.13 = s32[4,1]{0,1:T(1,128)} copy(s32[4,1]{0,1:T(1,128)S(1)} %bitcast.19) | data formatting | bytes 32
Async XLA Ops:
  26.5 1.4 %copy-start = (s32[1,4]{1,0:T(1,128)S(1)}, s32[1,4]{1,0:T(1,128)}, u32[]{:S(2)}) copy-start(s32[1,4]{1,0:T(1,128)} %get-tuple-element.5) | copy-start | bytes 52
